TPU v7x, 256 devices: a whole 4x4x8 slice. The times are simulated.
256 devices in a mesh: rep: 8 (over y, core), ep: 32 (over x, z).
Axes of the slice: x: 4, y: 4, z: 8, core: 2. Of those that a mesh axis runs over, the one named last changes fastest.
Arguments:
- tokens: bfloat16 [32768, 1024], P(('rep', 'ep')), may hold values from -6 to 6
- expert_ids: int32 [32768, 8], P(('rep', 'ep')), may hold values from 0 to 63, all different within a row; in each aligned block of 128 rows (0 to 127, 128 to 255, ...) at most 24 rows name the same one
- route_weights: float32 [32768, 8], P(('rep', 'ep')), may hold values from 0.03 to 0.5
- out_grad: bfloat16 [32768, 1024], P(('rep', 'ep')), may hold values from -4 to 4
- gate_weight: bfloat16 [64, 1024, 384], P('ep'), may hold values from -0.1875 to 0.1875
- up_weight: bfloat16 [64, 1024, 384], P('ep'), may hold values from -0.1875 to 0.1875
- down_weight: bfloat16 [64, 384, 1024], P('ep'), may hold values from -0.3125 to 0.3125
Outputs:
- layer_out: bfloat16 [32768, 1024], P(('rep', 'ep'))
- token_grad: bfloat16 [32768, 1024], P(('rep', 'ep'))
- route_grad: float32 [32768, 8], P(('rep', 'ep'))
- gate_weight_grad: float32 [64, 1024, 384], P('ep', 'rep')
- up_weight_grad: float32 [64, 1024, 384], P('ep', 'rep')
- down_weight_grad: float32 [64, 384, 1024], P('ep', 'rep')
Inputs may be any that keep to these rules, and one draw needn't show every extreme that they name: `expert_ids`: each row names 8 different experts. Among the rows of one device (an aligned block of 128 rows) no expert is named more than 24 times, and in every draw some expert is named exactly 24 times by the rows of some device.
All inputs are finite; a program needn't handle non-finite values.
Results may differ from a plain program's by a relative error of at most 0.014.
Values may be sent and summed in bfloat16 or wider, within the bound.
A program may use at most 128 MiB of HBM per device.

v0:
```python
import jax
import jax.numpy as jnp
from jax import lax
from jax.sharding import PartitionSpec as P


def silu_parts(gate_pre):
    sigmoid_gate = jax.nn.sigmoid(gate_pre)
    return (gate_pre * sigmoid_gate, sigmoid_gate * (1.0 + gate_pre * (1.0 - sigmoid_gate)))


def expert_forward(expert_in, gate_weight, up_weight, down_weight):
    gate_pre = jnp.einsum(
        "esnd,edf->esnf", expert_in, gate_weight, preferred_element_type=jnp.float32
    )
    up_pre = jnp.einsum("esnd,edf->esnf", expert_in, up_weight, preferred_element_type=jnp.float32)
    silu_gate, silu_slope = silu_parts(gate_pre)
    hidden = (silu_gate * up_pre).astype(jnp.bfloat16)
    expert_out = jnp.einsum(
        "esnf,efd->esnd", hidden, down_weight, preferred_element_type=jnp.float32
    ).astype(jnp.bfloat16)
    return (gate_pre, up_pre, hidden, expert_out)


def expert_backward(out_rows, gate_pre, up_pre, gate_weight, up_weight, down_weight):
    hidden_grad = jnp.einsum(
        "esnd,efd->esnf", out_rows, down_weight, preferred_element_type=jnp.float32
    )
    silu_gate, silu_slope = silu_parts(gate_pre)
    gate_delta = (hidden_grad * up_pre * silu_slope).astype(jnp.bfloat16)
    up_delta = (hidden_grad * silu_gate).astype(jnp.bfloat16)
    in_grads = jnp.einsum(
        "esnf,edf->esnd", gate_delta, gate_weight, preferred_element_type=jnp.float32
    ) + jnp.einsum("esnf,edf->esnd", up_delta, up_weight, preferred_element_type=jnp.float32)
    return (gate_delta, up_delta, in_grads.astype(jnp.bfloat16))


def per_device(tokens, expert_ids, route_weights, out_grad, gate_weight, up_weight, down_weight):
    tok_rows, model_width = tokens.shape
    top_count = expert_ids.shape[1]
    local_experts = gate_weight.shape[0]
    peer_count = lax.axis_size("ep")
    experts = local_experts * peer_count
    capacity = 3 * tok_rows * top_count // (2 * experts)
    slot_total = local_experts * peer_count * capacity
    flat_ids = expert_ids.reshape(-1)
    columns = jnp.arange(experts, dtype=jnp.int32)
    onehot = (flat_ids[:, None] == columns[None, :]).astype(jnp.int32)
    slot_rank = jnp.sum((jnp.cumsum(onehot, axis=0) - 1) * onehot, axis=1)
    target = (
        flat_ids % local_experts * peer_count + flat_ids // local_experts
    ) * capacity + slot_rank
    source = jnp.arange(tok_rows * top_count, dtype=jnp.int32) // top_count

    def pack_rows(pair_rows):
        filled = jnp.zeros((slot_total, model_width), jnp.bfloat16).at[target].set(pair_rows)
        return filled.reshape(local_experts, peer_count, capacity, model_width)

    def unpack_rows(returned):
        return returned.reshape(slot_total, model_width)[target].reshape(
            tok_rows, top_count, model_width
        )

    sent_tokens = pack_rows(tokens[source])
    scaled = (route_weights[:, :, None] * out_grad[:, None, :]).astype(jnp.bfloat16)
    sent_grads = pack_rows(scaled.reshape(tok_rows * top_count, model_width))
    expert_in = lax.all_to_all(sent_tokens, "ep", split_axis=1, concat_axis=1, tiled=True)
    gate_pre, up_pre, hidden, expert_out = expert_forward(
        expert_in, gate_weight, up_weight, down_weight
    )
    returned = lax.all_to_all(expert_out, "ep", split_axis=1, concat_axis=1, tiled=True)
    returned, expert_in, gate_pre, up_pre, hidden = (returned, expert_in, gate_pre, up_pre, hidden)
    out_rows = lax.all_to_all(sent_grads, "ep", split_axis=1, concat_axis=1, tiled=True)
    gate_delta, up_delta, in_grads = expert_backward(
        out_rows, gate_pre, up_pre, gate_weight, up_weight, down_weight
    )
    in_returned = lax.all_to_all(in_grads, "ep", split_axis=1, concat_axis=1, tiled=True)
    grad_down = jnp.einsum("esnf,esnd->efd", hidden, out_rows, preferred_element_type=jnp.float32)
    grad_gate = jnp.einsum(
        "esnd,esnf->edf", expert_in, gate_delta, preferred_element_type=jnp.float32
    )
    grad_up = jnp.einsum("esnd,esnf->edf", expert_in, up_delta, preferred_element_type=jnp.float32)
    gate_share, up_share, down_share = (
        lax.psum_scatter(
            grad_gate.astype(jnp.bfloat16), "rep", scatter_dimension=1, tiled=True
        ).astype(jnp.float32),
        lax.psum_scatter(
            grad_up.astype(jnp.bfloat16), "rep", scatter_dimension=1, tiled=True
        ).astype(jnp.float32),
        lax.psum_scatter(
            grad_down.astype(jnp.bfloat16), "rep", scatter_dimension=1, tiled=True
        ).astype(jnp.float32),
    )
    out_pairs = unpack_rows(returned)
    layer_out = jnp.sum(route_weights[:, :, None] * out_pairs, axis=1).astype(jnp.bfloat16)
    route_grad = jnp.einsum("td,tkd->tk", out_grad, out_pairs, preferred_element_type=jnp.float32)
    token_grad = jnp.sum(unpack_rows(in_returned).astype(jnp.float32), axis=1).astype(jnp.bfloat16)
    return (layer_out, token_grad, route_grad, gate_share, up_share, down_share)


def solution(mesh):
    return jax.shard_map(
        per_device,
        mesh=mesh,
        in_specs=(
            P(("rep", "ep"), None),
            P(("rep", "ep"), None),
            P(("rep", "ep"), None),
            P(("rep", "ep"), None),
            P("ep", None, None),
            P("ep", None, None),
            P("ep", None, None),
        ),
        out_specs=(
            P(("rep", "ep"), None),
            P(("rep", "ep"), None),
            P(("rep", "ep"), None),
            P("ep", "rep", None),
            P("ep", "rep", None),
            P("ep", "rep", None),
        ),
        check_vma=False,
    )
```

profile of v0, /device:TPU:16, one launch (start us, length us, event | category | flops | bytes accessed | tf_op | source)
XLA Modules:
  0.0 409.4 jit_solution(5811312368689597913)
XLA Ops:
  7.2 0.9 copy.51
  8.1 0.1 eq.31
  8.2 0.1 eq.27
  8.3 0.1 reshape.221
  8.4 18.0 %reduce-window.6 = s32[64,8,128]{2,1,0:T(8,128)S(1)} reduce-window(s32[64,8,128]{2,1,0:T(8,128)S(1)} %fusion.34, s32[]{:T(128)} %constant.50.clone.1), window={size=1x1x128 pad=0_0x0_0x127_0}, to_apply=%region_0.0 | reduce-window | flops 8323072 | bytes 524292 | tf_op jit(solution)/shard_map/reduce-window
  26.4 0.1 slice.14
  26.6 0.1 copy.54
  26.8 0.1 add_add_fusion
  27.1 16.8 %scatter_custom_fusion = bf16[1536,1024]{1,0:T(8,128)(2,1)} fusion(s32[1024]{0:T(1024)S(1)} %bitcast.80, bf16[128,1024]{1,0:T(8,128)(2,1)} %param.7, s32[1024]{0:T(1024)S(1)} %broadcast_clamp_fusion.1, bf16[]{:T(256)} %constant.49.clone.1), kind=kCustom, calls=%fused_computation.30 | custom fusion | bytes 3146240 | tf_op jit(solution)/shard_map/scatter | solution.py:56
  43.9 4.0 copy.56
  47.9 12.0 %all-to-all-start = ((bf16[2,32,24,1024]{3,2,0,1:T(8,128)(2,1)}), bf16[2,32,24,1024]{3,2,0,1:T(8,128)(2,1)}, u32[]{:S(2)}, u32[]{:S(2)}) async-start(bf16[2,32,24,1024]{3,2,0,1:T(8,128)(2,1)} %copy.56), calls=%async_computation | async-start | bytes 6291456 | tf_op jit(solution)/shard_map/all_to_all | solution.py:67
  60.0 0.1 copy.50
  60.1 0.1 mul.86
  60.2 7.8 %scatter_custom_fusion.1 = bf16[1536,1024]{1,0:T(8,128)(2,1)} fusion(s32[1024]{0:T(1024)S(1)} %bitcast.81, f32[128,1024]{1,0:T(8,128)S(1)} %convert_element_type.59, f32[1024]{0:T(1024)S(1)} %mul.86, bf16[]{:T(256)} %constant.49.clone.1), kind=kCustom, calls=%fused_computation.26 | custom fusion | flops 2097152 | bytes 3674114 | tf_op jit(solution)/shard_map/scatter | solution.py:56
  68.0 4.0 copy.62
  72.0 62.6 %all-to-all-done = bf16[2,32,24,1024]{3,2,0,1:T(8,128)(2,1)} async-done(((bf16[2,32,24,1024]{3,2,0,1:T(8,128)(2,1)}), bf16[2,32,24,1024]{3,2,0,1:T(8,128)(2,1)}, u32[]{:S(2)}, u32[]{:S(2)}) %all-to-all-start) | async-done | bytes 3145760 | tf_op jit(solution)/shard_map/all_to_all | solution.py:67
  134.6 6.0 %all-to-all-start.2 = ((bf16[2,32,24,1024]{3,2,0,1:T(8,128)(2,1)}), bf16[2,32,24,1024]{3,2,0,1:T(8,128)(2,1)}, u32[]{:S(2)}, u32[]{:S(2)}) async-start(bf16[2,32,24,1024]{3,2,0,1:T(8,128)(2,1)} %copy.62), calls=%async_computation.2 | async-start | bytes 6291456 | tf_op jit(solution)/shard_map/all_to_all | solution.py:73
  140.6 5.3 %fusion.5 = f32[2,32,24,384]{3,2,1,0:T(8,128)} fusion(bf16[2,32,24,1024]{3,2,0,1:T(8,128)(2,1)} %all-to-all-done, bf16[2,1024,384]{2,1,0:T(8,128)(2,1)S(1)} %copy-done.2), kind=kOutput, calls=%fused_computation.16 | convolution fusion | flops 1207959552 | bytes 7077888 | tf_op jit(solution)/shard_map/esnd,edf->esnf/dot_general | solution.py:16
  145.9 5.2 %fusion.7 = f32[2,32,24,384]{3,2,1,0:T(8,128)} fusion(bf16[2,32,24,1024]{3,2,0,1:T(8,128)(2,1)} %all-to-all-done, bf16[2,1024,384]{2,1,0:T(8,128)(2,1)S(1)} %copy-done.3), kind=kOutput, calls=%fused_computation.18 | convolution fusion | flops 1207959552 | bytes 7077888 | tf_op jit(solution)/shard_map/esnd,edf->esnf/dot_general | solution.py:13
  151.0 64.1 %all-to-all-done.2 = bf16[2,32,24,1024]{3,2,0,1:T(8,128)(2,1)} async-done(((bf16[2,32,24,1024]{3,2,0,1:T(8,128)(2,1)}), bf16[2,32,24,1024]{3,2,0,1:T(8,128)(2,1)}, u32[]{:S(2)}, u32[]{:S(2)}) %all-to-all-start.2) | async-done | bytes 3145760 | tf_op jit(solution)/shard_map/all_to_all | solution.py:73
  215.1 7.2 %multiply_convert_fusion = (bf16[2,32,24,384]{3,2,1,0:T(8,128)(2,1)}, bf16[2,32,24,384]{3,2,1,0:T(8,128)(2,1)}, bf16[2,32,24,384]{3,2,1,0:T(8,128)(2,1)S(1)}) fusion(f32[2,32,24,384]{3,2,1,0:T(8,128)} %fusion.7, f32[2,32,24,384]{3,2,1,0:T(8,128)} %fusion.5, bf16[2,384,1024]{2,1,0:T(8,128)(2,1)S(1)} %copy-done, bf16[2,32,24,1024]{3,2,0,1:T(8,128)(2,1)} %all-to-all-done.2), kind=kOutput, calls=%fused_computation.20 | convolution fusion | flops 1216806912 | bytes 12976128 | tf_op jit(solution)/shard_map/esnd,efd->esnf/dot_general | solution.py:26
  222.4 1.8 convolution_convert_fusion
  224.2 2.1 copy.59
  226.3 5.9 %all-to-all-start.1 = ((bf16[2,32,24,1024]{3,2,0,1:T(8,128)(2,1)}), bf16[2,32,24,1024]{3,2,0,1:T(8,128)(2,1)}, u32[]{:S(2)}, u32[]{:S(2)}) async-start(bf16[2,32,24,1024]{3,2,0,1:T(8,128)(2,1)} %copy.59), calls=%async_computation.1 | async-start | bytes 6291456 | tf_op jit(solution)/shard_map/all_to_all | solution.py:71
  232.3 4.9 %bitcast_convert_fusion = bf16[2,384,1024]{2,1,0:T(8,128)(2,1)} fusion(bf16[2,32,24,384]{3,2,1,0:T(8,128)(2,1)} %copy-done.10, bf16[2,32,24,1024]{3,2,0,1:T(8,128)(2,1)} %all-to-all-done.2), kind=kOutput, calls=%fused_computation.9 | convolution fusion | flops 1208745984 | bytes 5898240 | tf_op jit(solution)/shard_map/esnf,esnd->efd/dot_general | solution.py:78
  237.3 0.2 reduce-scatter.6.cloned.1.call-start
  237.5 4.9 %bitcast_convert_fusion.1 = bf16[2,1024,384]{2,1,0:T(8,128)(2,1)} fusion(bf16[2,32,24,1024]{3,2,0,1:T(8,128)(2,1)} %all-to-all-done, bf16[2,32,24,384]{3,2,1,0:T(8,128)(2,1)S(1)} %copy-done.6), kind=kOutput, calls=%fused_computation.10 | convolution fusion | flops 1208745984 | bytes 5898240 | tf_op jit(solution)/shard_map/esnd,esnf->edf/dot_general | solution.py:82
  242.4 1.4 copy-done.4
  243.8 3.2 fusion.22
  247.0 1.9 add_convert_fusion
  248.9 1.9 copy.64
  250.8 55.8 %all-to-all-done.1 = bf16[2,32,24,1024]{3,2,0,1:T(8,128)(2,1)} async-done(((bf16[2,32,24,1024]{3,2,0,1:T(8,128)(2,1)}), bf16[2,32,24,1024]{3,2,0,1:T(8,128)(2,1)}, u32[]{:S(2)}, u32[]{:S(2)}) %all-to-all-start.1) | async-done | bytes 3145760 | tf_op jit(solution)/shard_map/all_to_all | solution.py:71
  306.6 5.8 %all-to-all-start.3 = ((bf16[2,32,24,1024]{3,2,0,1:T(8,128)(2,1)}), bf16[2,32,24,1024]{3,2,0,1:T(8,128)(2,1)}, u32[]{:S(2)}, u32[]{:S(2)}) async-start(bf16[2,32,24,1024]{3,2,0,1:T(8,128)(2,1)} %copy.64), calls=%async_computation.3 | async-start | bytes 6291456 | tf_op jit(solution)/shard_map/all_to_all | solution.py:77
  312.4 0.3 reduce-scatter.4.cloned.1.call-start
  312.7 4.9 %bitcast_convert_fusion.2 = bf16[2,1024,384]{2,1,0:T(8,128)(2,1)} fusion(bf16[2,32,24,1024]{3,2,0,1:T(8,128)(2,1)} %all-to-all-done, bf16[2,32,24,384]{3,2,1,0:T(8,128)(2,1)S(1)} %copy-done.5), kind=kOutput, calls=%fused_computation.11 | convolution fusion | flops 1208745984 | bytes 5898240 | tf_op jit(solution)/shard_map/esnd,esnf->edf/dot_general | solution.py:79
  317.6 1.7 convert_element_type.69
  319.4 1.7 convert_element_type.67
  321.1 28.3 %reduce-scatter.4.cloned.1.call-done = bf16[2,128,384]{2,1,0:T(8,128)(2,1)} async-done(((bf16[2,1024,384]{2,1,0:T(8,128)(2,1)}), bf16[2,128,384]{2,1,0:T(8,128)(2,1)}) %reduce-scatter.4.cloned.1.call-update) | async-done | bytes 196624 | tf_op jit(solution)/shard_map/reduce_scatter | solution.py:84
  349.3 1.7 convert_element_type.65
  351.0 3.9 copy.60
  355.0 8.3 %gather_fusion = bf16[1024,1024]{1,0:T(8,128)(2,1)} fusion(bf16[1536,1024]{1,0:T(8,128)(2,1)} %bitcast.73, s32[1024]{0:T(1024)S(1)} %broadcast_clamp_fusion), kind=kCustom, calls=%fused_computation.1 | custom fusion | bytes 4198400 | tf_op jit(solution)/shard_map/gather | solution.py:60
  363.3 2.8 fusion.12
  366.1 0.7 copy.73
  366.8 3.7 multiply_reduce_fusion
  370.4 16.2 %all-to-all-done.3 = bf16[2,32,24,1024]{3,2,0,1:T(8,128)(2,1)} async-done(((bf16[2,32,24,1024]{3,2,0,1:T(8,128)(2,1)}), bf16[2,32,24,1024]{3,2,0,1:T(8,128)(2,1)}, u32[]{:S(2)}, u32[]{:S(2)}) %all-to-all-start.3) | async-done | bytes 3145760 | tf_op jit(solution)/shard_map/all_to_all | solution.py:77
  386.6 3.9 copy.65
  390.5 8.4 %gather_fusion.1 = bf16[1024,1024]{1,0:T(8,128)(2,1)} fusion(bf16[1536,1024]{1,0:T(8,128)(2,1)} %bitcast.72, s32[1024]{0:T(1024)S(1)} %broadcast_clamp_fusion), kind=kCustom, calls=%fused_computation.2 | custom fusion | bytes 4198400 | tf_op jit(solution)/shard_map/gather | solution.py:60
  399.0 3.7 bitcast_reduce_fusion
  (37 shorter events, 0.5 us)
Async XLA Ops:
  7.2 208.0 %copy-start = (bf16[2,384,1024]{2,1,0:T(8,128)(2,1)S(1)}, bf16[2,384,1024]{2,1,0:T(8,128)(2,1)}, u32[]{:S(2)}) copy-start(bf16[2,384,1024]{2,1,0:T(8,128)(2,1)} %param.13) | copy-start | bytes 4718596
  47.9 12.0 %copy-start.9 = (f32[128,8]{0,1:T(8,128)S(1)}, f32[128,8]{0,1:T(8,128)}, u32[]{:S(2)}) copy-start(f32[128,8]{0,1:T(8,128)} %param.9) | copy-start | bytes 12292
  47.9 12.2 %copy-start.8 = (bf16[128,1024]{1,0:T(8,128)(2,1)S(1)}, bf16[128,1024]{1,0:T(8,128)(2,1)}, u32[]{:S(2)}) copy-start(bf16[128,1024]{1,0:T(8,128)(2,1)} %param.10) | copy-start | bytes 786436
  47.9 86.7 %all-to-all-start = ((bf16[2,32,24,1024]{3,2,0,1:T(8,128)(2,1)}), bf16[2,32,24,1024]{3,2,0,1:T(8,128)(2,1)}, u32[]{:S(2)}, u32[]{:S(2)}) async-start(bf16[2,32,24,1024]{3,2,0,1:T(8,128)(2,1)} %copy.56), calls=%async_computation | async-start | bytes 6291456 | tf_op jit(solution)/shard_map/all_to_all | solution.py:67
  72.0 68.6 %copy-start.2 = (bf16[2,1024,384]{2,1,0:T(8,128)(2,1)S(1)}, bf16[2,1024,384]{2,1,0:T(8,128)(2,1)}, u32[]{:S(2)}) copy-start(bf16[2,1024,384]{2,1,0:T(8,128)(2,1)} %param.12) | copy-start | bytes 4718596
  134.6 80.5 %all-to-all-start.2 = ((bf16[2,32,24,1024]{3,2,0,1:T(8,128)(2,1)}), bf16[2,32,24,1024]{3,2,0,1:T(8,128)(2,1)}, u32[]{:S(2)}, u32[]{:S(2)}) async-start(bf16[2,32,24,1024]{3,2,0,1:T(8,128)(2,1)} %copy.62), calls=%async_computation.2 | async-start | bytes 6291456 | tf_op jit(solution)/shard_map/all_to_all | solution.py:73
  140.6 5.3 %copy-start.3 = (bf16[2,1024,384]{2,1,0:T(8,128)(2,1)S(1)}, bf16[2,1024,384]{2,1,0:T(8,128)(2,1)}, u32[]{:S(2)}) copy-start(bf16[2,1024,384]{2,1,0:T(8,128)(2,1)} %param.11) | copy-start | bytes 4718596
  222.4 1.8 copy-start.10
  226.3 80.3 %all-to-all-start.1 = ((bf16[2,32,24,1024]{3,2,0,1:T(8,128)(2,1)}), bf16[2,32,24,1024]{3,2,0,1:T(8,128)(2,1)}, u32[]{:S(2)}, u32[]{:S(2)}) async-start(bf16[2,32,24,1024]{3,2,0,1:T(8,128)(2,1)} %copy.59), calls=%async_computation.1 | async-start | bytes 6291456 | tf_op jit(solution)/shard_map/all_to_all | solution.py:71
  232.3 5.2 %copy-start.6 = (bf16[2,32,24,384]{3,2,1,0:T(8,128)(2,1)S(1)}, bf16[2,32,24,384]{3,2,1,0:T(8,128)(2,1)}, u32[]{:S(2)}) copy-start(bf16[2,32,24,384]{3,2,1,0:T(8,128)(2,1)} %get-tuple-element.6) | copy-start | bytes 3538948
  232.3 85.3 %reduce-scatter.8.cloned.1.call-start = ((), (), s32[]{:S(2)}) async-start(), calls=%async_computation.9 | async-start | bytes 1769472 | tf_op jit(solution)/shard_map/reduce_scatter | solution.py:90
  237.3 82.1 %reduce-scatter.6.cloned.1.call-start = ((), (), s32[]{:S(2)}) async-start(), calls=%async_computation.8 | async-start | bytes 1769472 | tf_op jit(solution)/shard_map/reduce_scatter | solution.py:87
  242.4 1.4 copy-start.4
  243.8 3.2 copy-start.7
  250.8 61.8 %copy-start.5 = (bf16[2,32,24,384]{3,2,1,0:T(8,128)(2,1)S(1)}, bf16[2,32,24,384]{3,2,1,0:T(8,128)(2,1)}, u32[]{:S(2)}) copy-start(bf16[2,32,24,384]{3,2,1,0:T(8,128)(2,1)} %get-tuple-element.7) | copy-start | bytes 3538948
  306.6 80.0 %all-to-all-start.3 = ((bf16[2,32,24,1024]{3,2,0,1:T(8,128)(2,1)}), bf16[2,32,24,1024]{3,2,0,1:T(8,128)(2,1)}, u32[]{:S(2)}, u32[]{:S(2)}) async-start(bf16[2,32,24,1024]{3,2,0,1:T(8,128)(2,1)} %copy.64), calls=%async_computation.3 | async-start | bytes 6291456 | tf_op jit(solution)/shard_map/all_to_all | solution.py:77
  312.4 37.0 %reduce-scatter.4.cloned.1.call-start = ((), (), s32[]{:S(2)}) async-start(), calls=%async_computation.7 | async-start | bytes 1769472 | tf_op jit(solution)/shard_map/reduce_scatter | solution.py:84
  390.5 12.2 %copy-start.1 = (bf16[2,384,1024]{2,1,0:T(8,128)(2,1)S(1)}, bf16[2,384,1024]{2,1,0:T(8,128)(2,1)}, u32[]{:S(2)}) copy-start(bf16[2,384,1024]{2,1,0:T(8,128)(2,1)} %param.13) | copy-start | bytes 4718596
Sparse Core Ops, SparseCore 0:
  237.4 31.5 reduce-scatter.7
  271.5 35.1 reduce-scatter.5
  317.7 31.5 reduce-scatter.3
where the time goes:
time: 417 us; the launch traced here: 409 us
  waiting for transfers between devices  227 us (54%)
  local copies, waits for them, and re-layouts  57.2 us (14%)
  matrix products  42.1 us (10%)
  other arithmetic  38.7 us (9%)
  starting transfers between devices  30.2 us (7%)
  between operations  14.2 us (3%)
    all_to_all x1, waiting for transfers between devices, per_device(): lax.all_to_all(sent_grads, 'ep', split_axis=1, concat_axis=1, tiled=True)  64.1 us
    all_to_all x1, waiting for transfers between devices, per_device(): lax.all_to_all(sent_tokens, 'ep', split_axis=1, concat_axis=1, tiled=True)  62.6 us
    all_to_all x1, waiting for transfers between devices, per_device(): lax.all_to_all(expert_out, 'ep', split_axis=1, concat_axis=1, tiled=True)  55.8 us
    reduce_scatter x1, waiting for transfers between devices, per_device(): lax.psum_scatter(grad_gate.astype(jnp.bfloat16), 'rep', scatter_dimension...  28.3 us
    another operation x2, other arithmetic  18 us
    scatter x1, local copies, waits for them, and re-layouts, pack_rows(): jnp.zeros((slot_total, model_width), jnp.bfloat16).at[target].set(pair_rows)  16.8 us
    gather x2, local copies, waits for them, and re-layouts, unpack_rows(): returned.reshape(slot_total, model_width)[target]  16.7 us
    all_to_all x1, waiting for transfers between devices, per_device(): lax.all_to_all(in_grads, 'ep', split_axis=1, concat_axis=1, tiled=True)  16.2 us
  transfers between devices with their start and end apart: 7, of which 5 were waited for; matrix products, arithmetic and copies ran while one was open for 17% of the time, Pallas kernels for 0%

commit v1 on v0

v1 whole, which is shorter than its diff:
```python
import jax
import jax.numpy as jnp
from jax import lax
from jax.experimental import pallas as pl
from jax.experimental.pallas import tpu as pltpu
from jax.sharding import PartitionSpec as P

MESH = pl.DeviceIdType.MESH
NX, NY, NZ, NC = 4, 4, 8, 2
TOK, D, FF, TOP, CAP = 128, 1024, 384, 8, 24
PAIR = 2 * TOK
SLOTS = 2 * CAP
ROWS = NZ * SLOTS
BF = jnp.bfloat16
F32 = jnp.float32
N_SEMS = 320


def nn(a, b):
    return lax.dot_general(a, b, (((1,), (0,)), ((), ())), preferred_element_type=F32)


def nt(a, b):
    return lax.dot_general(a, b, (((1,), (1,)), ((), ())), preferred_element_type=F32)


def tn(a, b):
    return lax.dot_general(a, b, (((0,), (0,)), ((), ())), preferred_element_type=F32)


class Net:
    def __init__(self, send, recv):
        self.send_sems, self.recv_sems, self.count = send, recv, 0
        self.pending = []

    def put(self, src, dst, dev):
        n = self.count
        self.count += 1
        copy = pltpu.make_async_remote_copy(
            src_ref=src,
            dst_ref=dst,
            send_sem=self.send_sems.at[n],
            recv_sem=self.recv_sems.at[n],
            device_id=dev,
            device_id_type=MESH,
        )
        copy.start()
        self.pending.append(copy)
        return n, dev

    def got(self, ticket, dst):
        n, dev = ticket
        pltpu.make_async_remote_copy(
            src_ref=dst,
            dst_ref=dst,
            send_sem=self.send_sems.at[n],
            recv_sem=self.recv_sems.at[n],
            device_id=dev,
            device_id_type=MESH,
        ).wait_recv()

    def drain(self):
        for copy in self.pending:
            copy.wait_send()
        self.pending = []


def kernel(
    tok, grd, meta, gw, uw, dw,
    lo, tg, rg, go, uo, do,
    tok_all, grd_all, meta_all, wg, wu, wd, xs, ors, pts, w8s,
    gg, gu, gd, sib_l, sib_t, rz, rp, rr,
    r0g, r0u, r0d, r1g, r1u, r1d, r2g, r2u, r2d, hg, hu, hd,
    send_sems, recv_sems, local_sems,
):
    rep, ep = lax.axis_index("rep"), lax.axis_index("ep")
    y, c = lax.div(rep, NC), lax.rem(rep, NC)
    x, z = lax.div(ep, NZ), lax.rem(ep, NZ)

    def up_x(d):
        return lax.rem(x + d + NX, NX)

    def up_y(d):
        return lax.rem(y + d + NY, NY)

    def up_z(d):
        return lax.rem(z + d + NZ, NZ)

    def dev(dx=0, dy=0, dz=0, dc=0):
        return (
            up_y(dy) * NC + lax.rem(c + dc, NC),
            up_x(dx) * NZ + up_z(dz),
        )

    column = [(dz, dc) for dz in range(NZ) for dc in range(NC) if dz or dc]
    barrier = pltpu.get_barrier_semaphore()
    partners = [dev(dz=dz, dc=dc) for dz, dc in column]
    partners += [dev(dx=1), dev(dx=-1), dev(dy=1), dev(dy=-1)]
    for partner in partners:
        pl.semaphore_signal(barrier, inc=1, device_id=partner, device_id_type=MESH)
    pl.semaphore_wait(barrier, len(partners))

    net = Net(send_sems, recv_sems)
    sib = dev(dc=1)
    other = lax.rem(c + 1, NC)

    arrays = ((tok, tok_all), (grd, grd_all))
    last = ((4, 3), (3, 4))
    ring = {}
    sibs = {}

    def z_send(way, a, s):
        d = 1 if way == 0 else -1
        src = arrays[a][0] if s == 0 else arrays[a][1].at[up_z(-d * s), c]
        dst = arrays[a][1].at[up_z(-d * s), c]
        ring[way, a, s] = net.put(src, dst, dev(dz=d))

    def z_take(way, a, s):
        d = 1 if way == 0 else -1
        where = up_z(-d * (s + 1))
        net.got(ring[way, a, s], arrays[a][1].at[where, c])
        if s + 1 < last[way][a]:
            z_send(way, a, s + 1)
        block = arrays[a][1].at[where, c]
        sibs[a, way, s] = (net.put(block, block, sib), arrays[a][1].at[where, other])

    metas = {}
    for dz, dc in column:
        metas[dz, dc] = net.put(meta, meta_all.at[z, c], dev(dz=dz, dc=dc))
    for a in range(2):
        for way in range(2):
            z_send(way, a, 0)
    rings_x = {}

    def x_send(name, way, s, src, dst):
        rings_x[name, way, s] = net.put(src, dst, dev(dx=1 if way == 0 else -1))

    quarter = ((uw, wu), (dw, wd))
    for h in range(2):
        for m in range(2):
            for way in range(2):
                x_send((m, h), way, 0, quarter[m][0].at[c, 2 * y + h], quarter[m][1].at[x, 2 * y + h])
    for h in range(2):
        for way in range(2):
            part = pl.ds(4 * h, 4)
            x_send((2, h), way, 0, gw.at[c, part], wg.at[x, part])
    for a in range(2):
        sibs[a, 0, -1] = (
            net.put(arrays[a][0], arrays[a][1].at[z, c], sib),
            arrays[a][1].at[z, other],
        )
    local = [
        pltpu.make_async_copy(src, dst, local_sems.at[i])
        for i, (src, dst) in enumerate(
            (
                (tok, tok_all.at[z, c]),
                (grd, grd_all.at[z, c]),
                (meta, meta_all.at[z, c]),
                (gw.at[c], wg.at[x]),
                (uw.at[c], wu.at[x]),
                (dw.at[c], wd.at[x]),
            )
        )
    ]
    for copy in local:
        copy.start()

    rings_y = {}

    def y_send(name, way, s, ref):
        rings_y[name, way, s] = net.put(ref, ref, dev(dy=1 if way == 0 else -1))

    def x_take_quarters(way):
        d = 1 if way == 0 else -1
        for h in range(2):
            for m in range(2):
                piece = quarter[m][1].at[up_x(-d), 2 * y + h]
                net.got(rings_x[(m, h), way, 0], piece)
                if h == way:
                    x_send((m, h), way, 1, piece, piece)
                for to in range(2):
                    y_send((m, h, -d), to, 0, piece)

    def x_take_far():
        for m in range(2):
            for way in range(2):
                piece = quarter[m][1].at[up_x(2), 2 * y + way]
                net.got(rings_x[(m, way), way, 1], piece)
                for to in range(2):
                    y_send((m, way, 2), to, 0, piece)

    def y_take(dx):
        for m in range(2):
            for way in range(2):
                d = 1 if way == 0 else -1
                for h in range(2):
                    piece = quarter[m][1].at[up_x(dx), 2 * up_y(-d) + h]
                    net.got(rings_y[(m, h, dx), way, 0], piece)
                    if h == way:
                        y_send((m, h, dx), way, 1, piece)

    def y_take_far(dx):
        for m in range(2):
            for way in range(2):
                piece = quarter[m][1].at[up_x(dx), 2 * up_y(2) + way]
                net.got(rings_y[(m, way, dx), way, 1], piece)

    def x_take_gate():
        for way in range(2):
            d = 1 if way == 0 else -1
            for h in range(2):
                piece = wg.at[up_x(-d), pl.ds(4 * h, 4)]
                net.got(rings_x[(2, h), way, 0], piece)
                if h == way:
                    x_send((2, h), way, 1, piece, piece)

    def x_take_gate_far():
        for way in range(2):
            piece = wg.at[up_x(2), pl.ds(4 * way, 4)]
            net.got(rings_x[(2, way), way, 1], piece)

    def z_step(a, s):
        for way in range(2):
            if s < last[way][a]:
                z_take(way, a, s)

    z_step(0, 0)
    x_take_quarters(0)
    x_take_quarters(1)
    z_step(1, 0)
    x_take_far()
    z_step(0, 1)
    y_take(-1)
    z_step(1, 1)
    y_take(1)
    z_step(0, 2)
    x_take_gate()
    y_take(2)
    z_step(1, 2)
    y_take_far(-1)
    y_take_far(1)
    z_step(0, 3)
    z_step(1, 3)
    y_take_far(2)
    x_take_gate_far()
    for dz, dc in column:
        net.got(metas[dz, dc], meta_all.at[up_z(-dz), lax.rem(c + dc, NC)])
    for ticket, dst in sibs.values():
        net.got(ticket, dst)
    for copy in local:
        copy.wait()
    net.drain()

    expert_col = lax.broadcasted_iota(jnp.int32, (8, PAIR), 0)
    names = jnp.where(expert_col < NX, 2 * (expert_col * NZ + z) + c, -1).astype(F32)
    t_row = lax.broadcasted_iota(jnp.int32, (PAIR, PAIR), 0)
    t_col = lax.broadcasted_iota(jnp.int32, (PAIR, PAIR), 1)
    same = (t_row < TOK) == (t_col < TOK)
    earlier = jnp.where((t_row < t_col) & same, 1.0, 0.0).astype(BF)
    base = jnp.where(lax.broadcasted_iota(jnp.int32, (8, PAIR), 1) < TOK, 0.0, float(CAP))
    slot_no = lax.broadcasted_iota(jnp.int32, (SLOTS, PAIR), 0).astype(F32)

    def ids_of(p):
        return jnp.concatenate([meta_all[p, 0, 0:8], meta_all[p, 1, 0:8]], axis=1)

    def pack(p, carry):
        ids = ids_of(p)
        weights = jnp.concatenate([meta_all[p, 0, 8:16], meta_all[p, 1, 8:16]], axis=1)
        hot, w8 = jnp.zeros((8, PAIR), F32), jnp.zeros((8, PAIR), F32)
        for k in range(TOP):
            hit = ids[k : k + 1] == names
            hot = hot + jnp.where(hit, 1.0, 0.0)
            w8 = w8 + jnp.where(hit, weights[k : k + 1], 0.0)
        rank = nn(hot.astype(BF), earlier)
        slot = jnp.where(hot > 0.5, rank + base, -1.0)
        rows, scales = [], []
        for i in range(NX):
            one = jnp.where(slot[i : i + 1] == slot_no, 1.0, 0.0)
            rows.append(one)
            scales.append(jnp.sum(one * w8[i : i + 1], axis=1, keepdims=True))
        pt = jnp.concatenate(rows, axis=0).astype(BF)
        scale = jnp.concatenate(scales, axis=0)
        pts[p] = pt
        w8s[p] = w8
        at = pl.ds(pl.multiple_of(p * SLOTS, 16), SLOTS)
        packed = nn(pt, tok_all[p].reshape(PAIR, D)).astype(BF)
        xs[:, at, :] = packed.reshape(NX, SLOTS, D)
        scaled = (nn(pt, grd_all[p].reshape(PAIR, D)) * scale).astype(BF)
        ors[:, at, :] = scaled.reshape(NX, SLOTS, D)
        return carry

    lax.fori_loop(0, NZ, pack, 0)

    def expert(i, carry):
        gate_w, up_w = wg[i].reshape(D, FF), wu[i].reshape(D, FF)
        down_w = wd[i].reshape(FF, D)
        rows, outs = xs[i], ors[i]
        gate_pre, up_pre = nn(rows, gate_w), nn(rows, up_w)
        sig = jax.nn.sigmoid(gate_pre)
        silu = gate_pre * sig
        slope = sig * (1.0 + gate_pre * (1.0 - sig))
        hidden = (silu * up_pre).astype(BF)
        hidden_grad = nt(outs, down_w)
        gate_delta = (hidden_grad * up_pre * slope).astype(BF)
        up_delta = (hidden_grad * silu).astype(BF)
        gg[i] = tn(rows, gate_delta).astype(BF).reshape(NY, 2, D // 8, FF)
        gu[i] = tn(rows, up_delta).astype(BF).reshape(NY, 2, D // 8, FF)
        gd[i] = tn(hidden, outs).astype(BF).reshape(NY, 2, FF // 8, D)
        xs[i] = nn(hidden, down_w).astype(BF)
        ors[i] = (nt(gate_delta, gate_w) + nt(up_delta, up_w)).astype(BF)
        return carry

    lax.fori_loop(0, NX, expert, 0)

    def combine(p, carry):
        at = pl.ds(pl.multiple_of(p * SLOTS, 16), SLOTS)
        ids = ids_of(p)
        pt, w8 = pts[p].astype(F32), w8s[p]
        outs = xs[:, at, :].reshape(NX * SLOTS, D)
        ins = ors[:, at, :].reshape(NX * SLOTS, D)
        weighted = jnp.concatenate(
            [pt[i * SLOTS : (i + 1) * SLOTS] * w8[i : i + 1] for i in range(NX)], axis=0
        ).astype(BF)
        dots = nt(outs, grd_all[p].reshape(PAIR, D)) * pt
        route = jnp.zeros((8, PAIR), F32)
        for i in range(NX):
            value = jnp.sum(dots[i * SLOTS : (i + 1) * SLOTS], axis=0, keepdims=True)
            route = route + jnp.where(ids == names[i : i + 1], value, 0.0)
        rp[p, 0] = route[:, :TOK]
        rp[p, 1] = route[:, TOK:]
        tok_all[p] = tn(weighted, outs).astype(BF).reshape(2, TOK, D)
        grd_all[p] = tn(pts[p], ins).astype(BF).reshape(2, TOK, D)
        return carry

    lax.fori_loop(0, NZ, combine, 0)

    parts = (tok_all, grd_all)
    outs = (lo, tg)
    sib_bufs = (sib_l, sib_t)
    order = [4, 3, 5, 2, 6, 1, 7, 0]
    sib_tickets = {}
    for off in order:
        for a in range(2):
            sib_tickets[a, off] = net.put(
                parts[a].at[up_z(off), other], sib_bufs[a].at[up_z(off)], sib
            )
    routes = {}
    for dz, dc in column:
        routes[dz, dc] = net.put(
            rp.at[up_z(dz), lax.rem(c + dc, NC)], rr.at[z, c], dev(dz=dz, dc=dc)
        )

    grads = (gg, gu, gd)
    bufs0, bufs1, bufs2 = (r0g, r0u, r0d), (r1g, r1u, r1d), (r2g, r2u, r2d)

    def view(g, h, p, q):
        return grads[g].at[p, q, h] if h == 0 else grads[g].at[q, p, h]

    def near(h, first, d):
        along_x = (h == 0) == first
        return dev(dx=d) if along_x else dev(dy=d)

    def step(h, first, d):
        along_x = (h == 0) == first
        return up_x(d) if along_x else up_y(d)

    def add(ref, *more):
        total = ref[...].astype(F32)
        for m in more:
            total = total + m[...].astype(F32)
        ref[...] = total.astype(BF)

    tickets = {}
    half = (pl.ds(0, 2), pl.ds(2, 2))
    signs = (1, -1)
    for h in range(2):
        for way in range(2):
            for g in range(3):
                tickets[0, h, way, g] = net.put(
                    view(g, h, step(h, True, 2), half[way]),
                    bufs0[g].at[h, way],
                    near(h, True, signs[way]),
                )
    for h in range(2):
        for way in range(2):
            for g in range(3):
                free = half[1 - way]
                tickets[1, h, way, g] = net.put(
                    view(g, h, step(h, True, signs[way]), free),
                    bufs1[g].at[h, way, free],
                    near(h, True, signs[way]),
                )

    def z_part(a, off):
        net.got(sib_tickets[a, off], sib_bufs[a].at[up_z(off)])

    chain = {}
    buf_no = {}
    for way in range(2):
        for a in range(2):
            for s in range(last[way][a]):
                buf_no[way, a, s] = len(buf_no)

    def z_pass(way, a, s):
        d = signs[way]
        off = d * (last[way][a] - s)
        z_part(a, off % NZ)
        block = parts[a].at[up_z(off), c]
        more = [sib_bufs[a].at[up_z(off)]]
        if s > 0:
            came = rz.at[buf_no[way, a, s - 1]]
            net.got(chain[way, a, s - 1], came)
            more.append(came)
        add(block, *more)
        chain[way, a, s] = net.put(block, rz.at[buf_no[way, a, s]], dev(dz=d))

    def grad_second(h):
        for way in range(2):
            for g in range(3):
                net.got(tickets[0, h, way, g], bufs0[g].at[h, way])
                mine = view(g, h, step(h, True, signs[way]), half[way])
                add(mine, bufs0[g].at[h, way])
                tickets[2, h, way, g] = net.put(
                    mine, bufs1[g].at[h, way, half[way]], near(h, True, signs[way])
                )

    far_way = ((0, 1, 0), (0, 1, 1))

    def grad_third(h):
        me = step(h, True, 0)
        for g in range(3):
            for way in range(2):
                net.got(tickets[1, h, way, g], bufs1[g].at[h, way, half[1 - way]])
                net.got(tickets[2, h, way, g], bufs1[g].at[h, way, half[way]])
            mine = view(g, h, me, pl.ds(0, 4))
            add(mine, bufs1[g].at[h, 0], bufs1[g].at[h, 1])
            way = far_way[h][g]
            tickets[3, h, g] = net.put(
                view(g, h, me, step(h, False, 2)),
                bufs2[g].at[h, 2],
                near(h, False, signs[way]),
            )
            tickets[4, h, g] = net.put(
                view(g, h, me, step(h, False, signs[1 - way])),
                bufs2[g].at[h, 1 - way],
                near(h, False, signs[1 - way]),
            )

    def grad_fourth(h):
        me = step(h, True, 0)
        for g in range(3):
            way = far_way[h][g]
            net.got(tickets[3, h, g], bufs2[g].at[h, 2])
            mine = view(g, h, me, step(h, False, signs[way]))
            add(mine, bufs2[g].at[h, 2])
            tickets[5, h, g] = net.put(
                mine, bufs2[g].at[h, way], near(h, False, signs[way])
            )

    for way in range(2):
        for a in range(2):
            if last[way][a] == 4:
                z_pass(way, a, 0)
    for way in range(2):
        for a in range(2):
            z_pass(way, a, last[way][a] - 3)
    grad_second(0)
    grad_second(1)
    for n in (2, 1):
        for way in range(2):
            for a in range(2):
                z_pass(way, a, last[way][a] - n)
    grad_third(0)
    grad_third(1)
    for a in range(2):
        z_part(a, 0)
        total = parts[a][z, c].astype(F32) + sib_bufs[a][z].astype(F32)
        for way in range(2):
            s = last[way][a] - 1
            came = rz.at[buf_no[way, a, s]]
            net.got(chain[way, a, s], came)
            total = total + came[...].astype(F32)
        outs[a][...] = total.astype(BF)
    total = rp[z, c]
    for dz, dc in column:
        came = rr.at[up_z(-dz), lax.rem(c + dc, NC)]
        net.got(routes[dz, dc], came)
        total = total + came[...]
    rg[...] = total
    grad_fourth(0)
    grad_fourth(1)

    finals = (go, uo, do)
    for h in range(2):
        for g in range(3):
            way = far_way[h][g]
            net.got(tickets[4, h, g], bufs2[g].at[h, 1 - way])
            net.got(tickets[5, h, g], bufs2[g].at[h, way])
    stage = (hg, hu, hd)
    hand = []
    for g in range(3):

        def whole(h):
            me = view(g, h, step(h, True, 0), step(h, False, 0))
            return (
                me[...].astype(F32)
                + bufs2[g][h, 0].astype(F32)
                + bufs2[g][h, 1].astype(F32)
            )

        both = (whole(0), whole(1))
        finals[g][c] = jnp.where(c == 0, both[0], both[1])
        away = jnp.where(c == 0, both[1], both[0])
        stage[g][0] = away.astype(BF)
        hand.append(net.put(stage[g].at[0], stage[g].at[1], sib))
    for g in range(3):
        net.got(hand[g], stage[g].at[1])
        finals[g][other] = stage[g][1].astype(F32)
    net.drain()


def per_device(tokens, expert_ids, route_weights, out_grad, gate_weight, up_weight, down_weight):
    meta = jnp.concatenate([expert_ids.astype(F32).T, route_weights.T], axis=0)
    gate_weight = gate_weight.reshape(2, 8, D // 8, FF)
    up_weight = up_weight.reshape(2, 8, D // 8, FF)
    down_weight = down_weight.reshape(2, 8, FF // 8, D)
    vmem = pl.BlockSpec(memory_space=pltpu.VMEM)
    hbm = pl.BlockSpec(memory_space=pl.ANY)
    wide, tall = (D // 8, FF), (FF // 8, D)
    piece = (wide, wide, tall)
    layer_out, token_grad, route_grad, gate_share, up_share, down_share = pl.pallas_call(
        kernel,
        out_shape=(
            jax.ShapeDtypeStruct((TOK, D), BF),
            jax.ShapeDtypeStruct((TOK, D), BF),
            jax.ShapeDtypeStruct((TOP, TOK), F32),
            jax.ShapeDtypeStruct((2, *wide), F32),
            jax.ShapeDtypeStruct((2, *wide), F32),
            jax.ShapeDtypeStruct((2, *tall), F32),
        ),
        in_specs=[vmem, vmem, vmem, hbm, hbm, hbm],
        out_specs=(vmem,) * 6,
        scratch_shapes=[
            pltpu.VMEM((NZ, NC, TOK, D), BF),
            pltpu.VMEM((NZ, NC, TOK, D), BF),
            pltpu.VMEM((NZ, NC, 16, TOK), F32),
            pltpu.VMEM((NX, 8, *wide), BF),
            pltpu.VMEM((NX, 8, *wide), BF),
            pltpu.VMEM((NX, 8, *tall), BF),
            pltpu.VMEM((NX, ROWS, D), BF),
            pltpu.VMEM((NX, ROWS, D), BF),
            pltpu.VMEM((NZ, NX * SLOTS, PAIR), BF),
            pltpu.VMEM((NZ, 8, PAIR), F32),
            pltpu.VMEM((NX, NY, 2, *wide), BF),
            pltpu.VMEM((NX, NY, 2, *wide), BF),
            pltpu.VMEM((NX, NY, 2, *tall), BF),
            pltpu.VMEM((NZ, TOK, D), BF),
            pltpu.VMEM((NZ, TOK, D), BF),
            pltpu.VMEM((14, TOK, D), BF),
            pltpu.VMEM((NZ, NC, TOP, TOK), F32),
            pltpu.VMEM((NZ, NC, TOP, TOK), F32),
            *[pltpu.VMEM((2, 2, 2, *s), BF) for s in piece],
            *[pltpu.VMEM((2, 2, 4, *s), BF) for s in piece],
            *[pltpu.VMEM((2, 3, *s), BF) for s in piece],
            *[pltpu.VMEM((2, *s), BF) for s in piece],
            pltpu.SemaphoreType.DMA((N_SEMS,)),
            pltpu.SemaphoreType.DMA((N_SEMS,)),
            pltpu.SemaphoreType.DMA((6,)),
        ],
        compiler_params=pltpu.CompilerParams(
            collective_id=0,
            has_side_effects=True,
            vmem_limit_bytes=62 * 1024 * 1024,
        ),
    )(tokens, out_grad, meta, gate_weight, up_weight, down_weight)
    return (layer_out, token_grad, route_grad.T, gate_share, up_share, down_share)


def solution(mesh):
    return jax.shard_map(
        per_device,
        mesh=mesh,
        in_specs=(
            P(("rep", "ep"), None),
            P(("rep", "ep"), None),
            P(("rep", "ep"), None),
            P(("rep", "ep"), None),
            P("ep", None, None),
            P("ep", None, None),
            P("ep", None, None),
        ),
        out_specs=(
            P(("rep", "ep"), None),
            P(("rep", "ep"), None),
            P(("rep", "ep"), None),
            P("ep", "rep", None),
            P("ep", "rep", None),
            P("ep", "rep", None),
        ),
        check_vma=False,
    )
```

time: 417 us -> 163 us (0.39)
  the two profiles are of different devices: /device:TPU:16 before, /device:TPU:1 now
where the time goes in v1:
time: 163 us
  Pallas kernels  152 us (93%)
  local copies, waits for them, and re-layouts  7.94 us (5%)
  other arithmetic  1.98 us (1%)
    pallas_call x1, Pallas kernels, per_device(): pl.pallas_call(kernel, out_shape=(jax.ShapeDtypeStruct((TOK, D), BF), jax...  152 us
    unnamed x10, local copies, waits for them, and re-layouts  7.94 us

profile of v1, /device:TPU:1, one launch (start us, length us, event | category | flops | bytes accessed | tf_op | source)
XLA Modules:
  0.0 162.9 jit_solution(4545248104470561705)
XLA Ops:
  0.6 0.7 convert_bitcast_fusion
  1.3 1.3 pad_maximum_fusion.meta
  2.6 152.4 %shard_map.118 = (bf16[128,1024]{1,0:T(8,128)(2,1)}, bf16[128,1024]{1,0:T(8,128)(2,1)}, f32[8,128]{1,0:T(8,128)}, f32[2,128,384]{2,1,0:T(8,128)}, f32[2,128,384]{2,1,0:T(8,128)}, /*index=5*/f32[2,48,1024]{2,1,0:T(8,128)}) custom-call(bf16[128,1024]{1,0:T(8,128)(2,1)} %tok.1, bf16[128,1024]{1,0:T(8,128)(2,1)} %grd.1, f32[16,128]{1,0:T(8,128)} %pad_maximum_fusion.meta, ...), custom_call_target="tpu_custom_call" | custom-call | tf_op jit(solution)/shard_map/pallas_call | solution.py:531
  155.0 0.0 copy-start.1
  155.0 0.0 copy-start
  155.0 1.7 %copy.19 = bf16[128,1024]{1,0:T(8,128)(2,1)} copy(bf16[128,1024]{1,0:T(8,128)(2,1)} %get-tuple-element.24) | data formatting | bytes 524288
  156.7 1.7 %copy.20 = bf16[128,1024]{1,0:T(8,128)(2,1)} copy(bf16[128,1024]{1,0:T(8,128)(2,1)} %get-tuple-element.25) | data formatting | bytes 524288
  158.4 1.3 copy.21
  159.7 1.8 %copy.22 = f32[2,128,384]{2,1,0:T(8,128)} copy(f32[2,128,384]{2,1,0:T(8,128)} %get-tuple-element.27) | data formatting | bytes 786432
  161.4 0.0 copy-done.1
  161.4 0.7 copy.23
  162.2 0.0 copy-done
  162.2 0.7 copy.24
Async XLA Ops:
  155.0 6.5 %copy-start.1 = (f32[2,128,384]{2,1,0:T(8,128)S(1)}, f32[2,128,384]{2,1,0:T(8,128)}, u32[]{:S(2)}) copy-start(f32[2,128,384]{2,1,0:T(8,128)} %get-tuple-element.28) | copy-start | bytes 1179652
  155.0 7.2 %copy-start = (f32[2,48,1024]{2,1,0:T(8,128)S(1)}, f32[2,48,1024]{2,1,0:T(8,128)}, u32[]{:S(2)}) copy-start(f32[2,48,1024]{2,1,0:T(8,128)} %get-tuple-element.29) | copy-start | bytes 1179652

commit v2 on v1

v2 whole, which is shorter than its diff:
```python
import jax
import jax.numpy as jnp
from jax import lax
from jax.experimental import pallas as pl
from jax.experimental.pallas import tpu as pltpu
from jax.sharding import PartitionSpec as P

MESH = pl.DeviceIdType.MESH
NX, NY, NZ, NC = 4, 4, 8, 2
TOK, D, FF, TOP, CAP = 128, 1024, 384, 8, 24
PAIR = 2 * TOK
SLOTS = 2 * CAP
ROWS = NZ * SLOTS
BF = jnp.bfloat16
F32 = jnp.float32


def nn(a, b):
    return lax.dot_general(a, b, (((1,), (0,)), ((), ())), preferred_element_type=F32)


def nt(a, b):
    return lax.dot_general(a, b, (((1,), (1,)), ((), ())), preferred_element_type=F32)


def tn(a, b):
    return lax.dot_general(a, b, (((0,), (0,)), ((), ())), preferred_element_type=F32)


class Net:
    def __init__(self, send, recv):
        self.send_sems, self.recv_sems = send, recv
        self.sent = self.count = 0
        self.pending = []

    def copy(self, src, dst, dev, out, into):
        return pltpu.make_async_remote_copy(
            src_ref=src,
            dst_ref=dst,
            send_sem=self.send_sems.at[out],
            recv_sem=self.recv_sems.at[into],
            device_id=dev,
            device_id_type=MESH,
        )

    def put(self, src, dst, dev):
        copy = self.copy(src, dst, dev, self.sent, self.count)
        copy.start()
        self.pending.append(copy)
        self.sent, self.count = self.sent + 1, self.count + 1
        return self.count - 1, dev

    def got(self, ticket, dst):
        into, dev = ticket
        self.copy(dst, dst, dev, 0, into).wait_recv()

    def drain(self):
        for copy in self.pending:
            copy.wait_send()
        self.pending, self.sent = [], 0


N_SEND, N_RECV = 110, 210
SIGNS = (1, -1)
LAST = ((4, 3), (3, 4))


def kernel(
    tok, grd, ids_in, weights_in, gw, uw, dw,
    lo, tg, rg, go, uo, do,
    tok_all, grd_all, meta_all, wg, wu, wd, xs, ors, igs, pts, w8s,
    gx, gd, sib_l, sib_t, sib_r, rz, zr, rp,
    xfx, xfd, xnx, xnd, yfx, yfd, ynx, ynd, sx, sd, hx, hd,
    send_sems, recv_sems, local_sems,
):
    rep, ep = lax.axis_index("rep"), lax.axis_index("ep")
    y, c = lax.div(rep, NC), lax.rem(rep, NC)
    x, z = lax.div(ep, NZ), lax.rem(ep, NZ)

    def up_x(d):
        return lax.rem(x + d + NX, NX)

    def up_y(d):
        return lax.rem(y + d + NY, NY)

    def up_z(d):
        return lax.rem(z + d + NZ, NZ)

    def dev(dx=0, dy=0, dz=0, dc=0):
        return (
            up_y(dy) * NC + lax.rem(c + dc, NC),
            up_x(dx) * NZ + up_z(dz),
        )

    sib = dev(dc=1)
    other = lax.rem(c + 1, NC)
    barrier = pltpu.get_barrier_semaphore()
    partners = [sib, dev(dx=1), dev(dx=-1), dev(dy=1), dev(dy=-1), dev(dz=1), dev(dz=-1)]
    for partner in partners:
        pl.semaphore_signal(barrier, inc=1, device_id=partner, device_id_type=MESH)
    meta_all[z, c, 0:8] = ids_in[...].astype(F32)
    meta_all[z, c, 8:16] = weights_in[...]
    pl.semaphore_wait(barrier, len(partners))
    net = Net(send_sems, recv_sems)

    blocks = (tok_all, grd_all)
    firsts = (tok, grd)
    ring, sibs = {}, {}

    def z_send(way, a, s):
        d = SIGNS[way]
        block = blocks[a].at[up_z(-d * s), c]
        src = firsts[a] if s == 0 else block
        ring[way, a, s] = net.put(src, block, dev(dz=d))
        if a == 0:
            note = meta_all.at[up_z(-d * s), c]
            ring[way, 2, s] = net.put(note, note, dev(dz=d))

    def z_step(a, s):
        for way in range(2):
            if s < LAST[way][a]:
                off = -SIGNS[way] * (s + 1)
                where = up_z(off)
                block = blocks[a].at[where, c]
                net.got(ring[way, a, s], block)
                if a == 0:
                    net.got(ring[way, 2, s], meta_all.at[where, c])
                if s + 1 < LAST[way][a]:
                    z_send(way, a, s + 1)
                share(a, off, block)

    def share(a, off, src):
        where = up_z(off)
        sibs[a, off % NZ] = net.put(src, blocks[a].at[where, c], sib)
        if a == 0:
            note = meta_all.at[where, c]
            sibs[2, off % NZ] = net.put(note, note, sib)

    for a in range(2):
        for way in range(2):
            z_send(way, a, 0)
    rings_x = {}

    def x_send(name, way, s, src, dst):
        rings_x[name, way, s] = net.put(src, dst, dev(dx=SIGNS[way]))

    quarter = ((uw, wu), (dw, wd))
    for h in range(2):
        for m in range(2):
            for way in range(2):
                x_send((m, h), way, 0, quarter[m][0].at[c, 2 * y + h], quarter[m][1].at[x, 2 * y + h])
    for h in range(2):
        for way in range(2):
            part = pl.ds(4 * h, 4)
            x_send((2, h), way, 0, gw.at[c, part], wg.at[x, part])
    for a in range(2):
        share(a, 0, firsts[a])
    local = [
        pltpu.make_async_copy(src, dst, local_sems.at[i])
        for i, (src, dst) in enumerate(
            (
                (tok, tok_all.at[z, c]),
                (grd, grd_all.at[z, c]),
                (gw.at[c], wg.at[x]),
                (uw.at[c], wu.at[x]),
                (dw.at[c], wd.at[x]),
            )
        )
    ]
    for copy in local:
        copy.start()

    rings_y = {}

    def y_send(name, way, s, ref):
        rings_y[name, way, s] = net.put(ref, ref, dev(dy=SIGNS[way]))

    def x_take_quarters(way):
        d = SIGNS[way]
        for h in range(2):
            for m in range(2):
                piece = quarter[m][1].at[up_x(-d), 2 * y + h]
                net.got(rings_x[(m, h), way, 0], piece)
                if h == way:
                    x_send((m, h), way, 1, piece, piece)
                for to in range(2):
                    y_send((m, h, -d), to, 0, piece)

    def x_take_far():
        for m in range(2):
            for way in range(2):
                piece = quarter[m][1].at[up_x(2), 2 * y + way]
                net.got(rings_x[(m, way), way, 1], piece)
                for to in range(2):
                    y_send((m, way, 2), to, 0, piece)

    def y_take(dx):
        for m in range(2):
            for way in range(2):
                for h in range(2):
                    piece = quarter[m][1].at[up_x(dx), 2 * up_y(-SIGNS[way]) + h]
                    net.got(rings_y[(m, h, dx), way, 0], piece)
                    if h == way:
                        y_send((m, h, dx), way, 1, piece)

    def y_take_far(dx):
        for m in range(2):
            for way in range(2):
                piece = quarter[m][1].at[up_x(dx), 2 * up_y(2) + way]
                net.got(rings_y[(m, way, dx), way, 1], piece)

    def x_take_gate():
        for way in range(2):
            for h in range(2):
                piece = wg.at[up_x(-SIGNS[way]), pl.ds(4 * h, 4)]
                net.got(rings_x[(2, h), way, 0], piece)
                if h == way:
                    x_send((2, h), way, 1, piece, piece)

    def x_take_gate_far():
        for way in range(2):
            piece = wg.at[up_x(2), pl.ds(4 * way, 4)]
            net.got(rings_x[(2, way), way, 1], piece)

    expert_col = lax.broadcasted_iota(jnp.int32, (8, PAIR), 0)
    names = jnp.where(expert_col < NX, 2 * (expert_col * NZ + z) + c, -1).astype(F32)
    t_row = lax.broadcasted_iota(jnp.int32, (PAIR, PAIR), 0)
    t_col = lax.broadcasted_iota(jnp.int32, (PAIR, PAIR), 1)
    same = (t_row < TOK) == (t_col < TOK)
    earlier = jnp.where((t_row < t_col) & same, 1.0, 0.0).astype(BF)
    base = jnp.where(lax.broadcasted_iota(jnp.int32, (8, PAIR), 1) < TOK, 0.0, float(CAP))
    slot_no = lax.broadcasted_iota(jnp.int32, (SLOTS, PAIR), 0).astype(F32)

    def ids_of(p):
        return jnp.concatenate([meta_all[p, 0, 0:8], meta_all[p, 1, 0:8]], axis=1)

    def pack(off):
        p = up_z(off)
        for a in range(2):
            net.got(sibs[a, off % NZ], blocks[a].at[p, other])
        net.got(sibs[2, off % NZ], meta_all.at[p, other])
        ids = ids_of(p)
        weights = jnp.concatenate([meta_all[p, 0, 8:16], meta_all[p, 1, 8:16]], axis=1)
        hot, w8 = jnp.zeros((8, PAIR), F32), jnp.zeros((8, PAIR), F32)
        for k in range(TOP):
            hit = ids[k : k + 1] == names
            hot = hot + jnp.where(hit, 1.0, 0.0)
            w8 = w8 + jnp.where(hit, weights[k : k + 1], 0.0)
        rank = nn(hot.astype(BF), earlier)
        slot = jnp.where(hot > 0.5, rank + base, -1.0)
        rows, scales = [], []
        for i in range(NX):
            one = jnp.where(slot[i : i + 1] == slot_no, 1.0, 0.0)
            rows.append(one)
            scales.append(jnp.sum(one * w8[i : i + 1], axis=1, keepdims=True))
        pt = jnp.concatenate(rows, axis=0).astype(BF)
        scale = jnp.concatenate(scales, axis=0)
        pts[p] = pt
        w8s[p] = w8
        at = pl.ds(pl.multiple_of(p * SLOTS, 16), SLOTS)
        packed = nn(pt, tok_all[p].reshape(PAIR, D)).astype(BF)
        xs[:, at, :] = packed.reshape(NX, SLOTS, D)
        scaled = (nn(pt, grd_all[p].reshape(PAIR, D)) * scale).astype(BF)
        ors[:, at, :] = scaled.reshape(NX, SLOTS, D)

    def expert(dx):
        i = up_x(dx)
        gate_w, up_w = wg[i].reshape(D, FF), wu[i].reshape(D, FF)
        down_w = wd[i].reshape(FF, D)
        rows, outs = xs[i], ors[i]
        gate_pre, up_pre = nn(rows, gate_w), nn(rows, up_w)
        sig = jax.nn.sigmoid(gate_pre)
        silu = gate_pre * sig
        slope = sig * (1.0 + gate_pre * (1.0 - sig))
        hidden = (silu * up_pre).astype(BF)
        hidden_grad = nt(outs, down_w)
        gate_delta = (hidden_grad * up_pre * slope).astype(BF)
        up_delta = (hidden_grad * silu).astype(BF)
        igs[i] = (nt(gate_delta, gate_w) + nt(up_delta, up_w)).astype(BF)
        expert_out = nn(hidden, down_w).astype(BF)
        wd[i] = expert_out.reshape(8, ROWS // 8, D)
        wg[i, 0:3] = hidden.reshape(3, TOK, FF)
        wu[i, 0:3] = gate_delta.reshape(3, TOK, FF)
        wu[i, 3:6] = up_delta.reshape(3, TOK, FF)

    def weight_grads(dx):
        i = up_x(dx)
        rows, outs = xs[i], ors[i]
        for m in range(2):
            delta = wu[i, 3 * m : 3 * m + 3].reshape(ROWS, FF)
            gx[i, :, :, m] = tn(rows, delta).astype(BF).reshape(NY, 2, TOK, FF)
        hidden = wg[i, 0:3].reshape(ROWS, FF)
        gd[i] = tn(hidden, outs).astype(BF).reshape(NY, 2, FF // 8, D)

    parts = (tok_all, grd_all)
    sib_bufs = (sib_l, sib_t)
    sib_tickets = {}

    def combine(off):
        p = up_z(off)
        ids = ids_of(p)
        pt, w8 = pts[p].astype(F32), w8s[p]
        outs = wd[:, p].reshape(NX * SLOTS, D)
        at = pl.ds(pl.multiple_of(p * SLOTS, 16), SLOTS)
        ins = igs[:, at, :].reshape(NX * SLOTS, D)
        weighted = jnp.concatenate(
            [pt[i * SLOTS : (i + 1) * SLOTS] * w8[i : i + 1] for i in range(NX)], axis=0
        ).astype(BF)
        dots = nt(outs, grd_all[p].reshape(PAIR, D)) * pt
        route = jnp.zeros((8, PAIR), F32)
        for i in range(NX):
            value = jnp.sum(dots[i * SLOTS : (i + 1) * SLOTS], axis=0, keepdims=True)
            route = route + jnp.where(ids == names[i : i + 1], value, 0.0)
        rp[p, 0] = route[:, :TOK]
        rp[p, 1] = route[:, TOK:]
        tok_all[p] = tn(weighted, outs).astype(BF).reshape(2, TOK, D)
        grd_all[p] = tn(pts[p], ins).astype(BF).reshape(2, TOK, D)
        for a in range(2):
            sib_tickets[a, off % NZ] = net.put(parts[a].at[p, other], sib_bufs[a].at[p], sib)
        sib_tickets[2, off % NZ] = net.put(rp.at[p, other], sib_r.at[p], sib)

    z_step(0, 0)
    x_take_quarters(0)
    x_take_quarters(1)
    for copy in local:
        copy.wait()
    z_step(1, 0)
    x_take_far()
    pack(0)
    z_step(0, 1)
    y_take(-1)
    pack(1)
    pack(-1)
    z_step(1, 1)
    y_take(1)
    z_step(0, 2)
    x_take_gate()
    y_take(2)
    pack(2)
    pack(-2)
    z_step(1, 2)
    y_take_far(-1)
    y_take_far(1)
    z_step(0, 3)
    pack(3)
    pack(-3)
    z_step(1, 3)
    y_take_far(2)
    x_take_gate_far()
    pack(4)
    net.drain()

    grads = (gx, gd)
    chain, tickets = {}, {}
    buf_no = {}
    for way in range(2):
        for a in range(2):
            for s in range(LAST[way][a]):
                buf_no[way, a, s] = len(buf_no)

    def add(ref, *more):
        total = ref[...].astype(F32)
        for m in more:
            total = total + m[...].astype(F32)
        ref[...] = total.astype(BF)

    def z_pass(way, a, s):
        d = SIGNS[way]
        off = d * (LAST[way][a] - s)
        where = up_z(off)
        net.got(sib_tickets[a, off % NZ], sib_bufs[a].at[where])
        block = parts[a].at[where, c]
        more = [sib_bufs[a].at[where]]
        if s > 0:
            came = rz.at[buf_no[way, a, s - 1]]
            net.got(chain[way, a, s - 1], came)
            more.append(came)
        add(block, *more)
        chain[way, a, s] = net.put(block, rz.at[buf_no[way, a, s]], dev(dz=d))
        if a == 0:
            net.got(sib_tickets[2, off % NZ], sib_r.at[where])
            route = rp[where, c] + sib_r[where]
            if s > 0:
                net.got(chain[way, 2, s - 1], zr.at[buf_no[way, 0, s - 1]])
                route = route + zr[buf_no[way, 0, s - 1]]
            rp[where, c] = route
            chain[way, 2, s] = net.put(
                rp.at[where, c], zr.at[buf_no[way, 0, s]], dev(dz=d)
            )

    half = (pl.ds(0, 2), pl.ds(2, 2))
    far_x, near_x = (xfx, xfd), (xnx, xnd)
    far_y, near_y = (yfx, yfd), (ynx, ynd)
    second = (sx, sd)

    def y_way(dx):
        return 0 if dx in (2, 1) else 1

    def grad_send(dx):
        i = up_x(dx)
        for g in range(2):
            if dx == 2:
                for way in range(2):
                    tickets["xf", way, g] = net.put(
                        grads[g].at[i, half[way], 0], far_x[g].at[way], dev(dx=SIGNS[way])
                    )
            elif dx:
                way = SIGNS.index(dx)
                free = half[1 - way]
                tickets["xa", way, g] = net.put(
                    grads[g].at[i, free, 0], near_x[g].at[way, free], dev(dx=dx)
                )
            way = y_way(dx)
            tickets["yf", dx, g] = net.put(
                grads[g].at[i, up_y(2), 1], far_y[g].at[dx % NX], dev(dy=SIGNS[way])
            )
            tickets["yn", dx, 1 - way, g] = net.put(
                grads[g].at[i, up_y(SIGNS[1 - way]), 1],
                near_y[g].at[dx % NX, 1 - way],
                dev(dy=SIGNS[1 - way]),
            )

    def x_pass(way):
        i = up_x(SIGNS[way])
        for g in range(2):
            net.got(tickets["xf", way, g], far_x[g].at[way])
            mine = grads[g].at[i, half[way], 0]
            add(mine, far_x[g].at[way])
            tickets["xb", way, g] = net.put(
                mine, near_x[g].at[way, half[way]], dev(dx=SIGNS[way])
            )

    def y_pass(dx):
        way = y_way(dx)
        for g in range(2):
            net.got(tickets["yf", dx, g], far_y[g].at[dx % NX])
            mine = grads[g].at[up_x(dx), up_y(SIGNS[way]), 1]
            add(mine, far_y[g].at[dx % NX])
            tickets["yn", dx, way, g] = net.put(
                mine, near_y[g].at[dx % NX, way], dev(dy=SIGNS[way])
            )

    def second_view(h, g, d):
        return grads[g].at[x, up_y(d), 0] if h == 0 else grads[g].at[up_x(d), y, 1]

    def second_dev(h, way):
        return dev(dy=SIGNS[way]) if h == 0 else dev(dx=SIGNS[way])

    def second_send(h, g):
        way = g
        tickets["sf", h, g] = net.put(
            second_view(h, g, 2), second[g].at[h, 2], second_dev(h, way)
        )
        tickets["sn", h, g, 1 - way] = net.put(
            second_view(h, g, SIGNS[1 - way]), second[g].at[h, 1 - way], second_dev(h, 1 - way)
        )

    def x_last():
        for g in range(2):
            for way in range(2):
                net.got(tickets["xa", way, g], near_x[g].at[way, half[1 - way]])
                net.got(tickets["xb", way, g], near_x[g].at[way, half[way]])
            add(grads[g].at[x, :, 0], near_x[g].at[0], near_x[g].at[1])
            second_send(0, g)

    def y_last():
        for g in range(2):
            for dx in (2, 1, -1, 0):
                for way in range(2):
                    net.got(tickets["yn", dx, way, g], near_y[g].at[dx % NX, way])
                near = near_y[g].at[dx % NX]
                add(grads[g].at[up_x(dx), y, 1], near.at[0], near.at[1])
            second_send(1, g)

    def second_pass(h):
        for g in range(2):
            way = g
            net.got(tickets["sf", h, g], second[g].at[h, 2])
            mine = second_view(h, g, SIGNS[way])
            add(mine, second[g].at[h, 2])
            tickets["sn", h, g, way] = net.put(
                mine, second[g].at[h, way], second_dev(h, way)
            )

    expert(2)
    weight_grads(2)
    grad_send(2)
    expert(1)
    expert(-1)
    expert(0)
    combine(4)
    combine(3)
    combine(-3)
    z_pass(0, 0, 0)
    z_pass(1, 1, 0)
    z_pass(0, 1, 0)
    z_pass(1, 0, 0)
    weight_grads(1)
    grad_send(1)
    weight_grads(-1)
    grad_send(-1)
    x_pass(0)
    x_pass(1)
    combine(2)
    combine(-2)
    z_pass(0, 0, 1)
    z_pass(1, 1, 1)
    weight_grads(0)
    grad_send(0)
    z_pass(0, 1, 1)
    z_pass(1, 0, 1)
    y_pass(2)
    y_pass(1)
    y_pass(-1)
    combine(1)
    combine(-1)
    z_pass(0, 0, 2)
    z_pass(1, 1, 2)
    y_pass(0)
    x_last()
    z_pass(0, 1, 2)
    z_pass(1, 0, 2)
    combine(0)
    y_last()
    z_pass(0, 0, 3)
    z_pass(1, 1, 3)
    second_pass(0)
    second_pass(1)

    results = (lo, tg)
    for a in range(2):
        net.got(sib_tickets[a, 0], sib_bufs[a].at[z])
        total = parts[a][z, c].astype(F32) + sib_bufs[a][z].astype(F32)
        for way in range(2):
            s = LAST[way][a] - 1
            came = rz.at[buf_no[way, a, s]]
            net.got(chain[way, a, s], came)
            total = total + came[...].astype(F32)
        results[a][...] = total.astype(BF)
    net.got(sib_tickets[2, 0], sib_r.at[z])
    total = rp[z, c] + sib_r[z]
    for way in range(2):
        no = buf_no[way, 0, LAST[way][0] - 1]
        net.got(chain[way, 2, LAST[way][0] - 1], zr.at[no])
        total = total + zr[no]
    rg[...] = total

    finals = ((go, uo), (do,))
    stage = (hx, hd)
    hand = []
    for g in range(2):
        both = []
        for h in range(2):
            for way in range(2):
                net.got(tickets["sn", h, g, way], second[g].at[h, way])
            both.append(
                second_view(h, g, 0)[...].astype(F32)
                + second[g][h, 0].astype(F32)
                + second[g][h, 1].astype(F32)
            )
        keep = jnp.where(c == 0, both[0], both[1])
        away = jnp.where(c == 0, both[1], both[0])
        stage[g][0] = away.astype(BF)
        hand.append(net.put(stage[g].at[0], stage[g].at[1], sib))
        if g == 0:
            go[c], uo[c] = keep[0], keep[1]
        else:
            do[c] = keep
    net.got(hand[0], hx.at[1])
    go[other] = hx[1, 0].astype(F32)
    uo[other] = hx[1, 1].astype(F32)
    net.got(hand[1], hd.at[1])
    do[other] = hd[1].astype(F32)
    net.drain()


def hand_out(*refs):
    n = len(refs) // 2
    copies = [
        pltpu.make_async_copy(refs[i], refs[n + i], refs[2 * n].at[i]) for i in range(n)
    ]
    for copy in copies:
        copy.start()
    for copy in copies:
        copy.wait()


def per_device(tokens, expert_ids, route_weights, out_grad, gate_weight, up_weight, down_weight):
    gate_weight = gate_weight.reshape(2, 8, D // 8, FF)
    up_weight = up_weight.reshape(2, 8, D // 8, FF)
    down_weight = down_weight.reshape(2, 8, FF // 8, D)
    vmem = pl.BlockSpec(memory_space=pltpu.VMEM)
    hbm = pl.BlockSpec(memory_space=pl.ANY)
    wide, tall = (D // 8, FF), (FF // 8, D)
    two = (2, *wide)
    out_shape = (
        jax.ShapeDtypeStruct((TOK, D), BF),
        jax.ShapeDtypeStruct((TOK, D), BF),
        jax.ShapeDtypeStruct((TOP, TOK), F32),
        jax.ShapeDtypeStruct((2, *wide), F32),
        jax.ShapeDtypeStruct((2, *wide), F32),
        jax.ShapeDtypeStruct((2, *tall), F32),
    )
    results = pl.pallas_call(
        kernel,
        out_shape=out_shape,
        in_specs=[vmem, vmem, vmem, vmem, hbm, hbm, hbm],
        out_specs=(vmem,) * 6,
        scratch_shapes=[
            pltpu.VMEM((NZ, NC, TOK, D), BF),
            pltpu.VMEM((NZ, NC, TOK, D), BF),
            pltpu.VMEM((NZ, NC, 16, TOK), F32),
            pltpu.VMEM((NX, 8, *wide), BF),
            pltpu.VMEM((NX, 8, *wide), BF),
            pltpu.VMEM((NX, 8, *tall), BF),
            pltpu.VMEM((NX, ROWS, D), BF),
            pltpu.VMEM((NX, ROWS, D), BF),
            pltpu.VMEM((NX, ROWS, D), BF),
            pltpu.VMEM((NZ, NX * SLOTS, PAIR), BF),
            pltpu.VMEM((NZ, 8, PAIR), F32),
            pltpu.VMEM((NX, NY, 2, *two), BF),
            pltpu.VMEM((NX, NY, 2, *tall), BF),
            pltpu.VMEM((NZ, TOK, D), BF),
            pltpu.VMEM((NZ, TOK, D), BF),
            pltpu.VMEM((NZ, TOP, TOK), F32),
            pltpu.VMEM((14, TOK, D), BF),
            pltpu.VMEM((14, TOP, TOK), F32),
            pltpu.VMEM((NZ, NC, TOP, TOK), F32),
            *[pltpu.VMEM((2, 2, *s), BF) for s in (two, tall)],
            *[pltpu.VMEM((2, 4, *s), BF) for s in (two, tall)],
            *[pltpu.VMEM((4, *s), BF) for s in (two, tall)],
            *[pltpu.VMEM((4, 2, *s), BF) for s in (two, tall)],
            *[pltpu.VMEM((2, 3, *s), BF) for s in (two, tall)],
            *[pltpu.VMEM((2, *s), BF) for s in (two, tall)],
            pltpu.SemaphoreType.DMA((N_SEND,)),
            pltpu.SemaphoreType.DMA((N_RECV,)),
            pltpu.SemaphoreType.DMA((5,)),
        ],
        compiler_params=pltpu.CompilerParams(
            collective_id=0,
            has_side_effects=True,
            vmem_limit_bytes=63 * 1024 * 1024,
        ),
    )(tokens, out_grad, expert_ids.T, route_weights.T, gate_weight, up_weight, down_weight)
    layer_out, token_grad, route_grad, gate_share, up_share, down_share = pl.pallas_call(
        hand_out,
        out_shape=out_shape,
        in_specs=[hbm] * 6,
        out_specs=(hbm,) * 6,
        scratch_shapes=[pltpu.SemaphoreType.DMA((6,))],
    )(*results)
    return (layer_out, token_grad, route_grad.T, gate_share, up_share, down_share)


def solution(mesh):
    return jax.shard_map(
        per_device,
        mesh=mesh,
        in_specs=(
            P(("rep", "ep"), None),
            P(("rep", "ep"), None),
            P(("rep", "ep"), None),
            P(("rep", "ep"), None),
            P("ep", None, None),
            P("ep", None, None),
            P("ep", None, None),
        ),
        out_specs=(
            P(("rep", "ep"), None),
            P(("rep", "ep"), None),
            P(("rep", "ep"), None),
            P("ep", "rep", None),
            P("ep", "rep", None),
            P("ep", "rep", None),
        ),
        check_vma=False,
    )
```

time: 163 us -> 186 us (1.14)
  Pallas kernels: 152 us -> 185 us
  local copies, waits for them, and re-layouts: 7.94 us -> 0 us
  other arithmetic: 1.98 us -> 0 us
    pallas_call x1 -> x2, Pallas kernels: 152 us -> 185 us  [the longest x1 132 us: per_device(): pl.pallas_call(kernel, out_shape=out_shape, in_specs=[vmem, vmem, vmem, v...]
    unnamed x10 -> x0, local copies, waits for them, and re-layouts: 7.94 us -> none
where the time goes in v2:
time: 186 us
  Pallas kernels  185 us (99%)
    pallas_call x1, Pallas kernels, per_device(): pl.pallas_call(kernel, out_shape=out_shape, in_specs=[vmem, vmem, vmem, v...  132 us
    pallas_call x1, Pallas kernels, per_device(): pl.pallas_call(hand_out, out_shape=out_shape, in_specs=[hbm] * 6, out_spe...  52.9 us

profile of v2, /device:TPU:1, one launch (start us, length us, event | category | flops | bytes accessed | tf_op | source)
XLA Modules:
  0.0 185.9 jit_solution(5856575666508610434)
XLA Ops:
  0.6 132.2 %shard_map.118 = (bf16[128,1024]{1,0:T(8,128)(2,1)}, bf16[128,1024]{1,0:T(8,128)(2,1)}, f32[8,128]{1,0:T(8,128)}, f32[2,128,384]{2,1,0:T(8,128)}, f32[2,128,384]{2,1,0:T(8,128)}, /*index=5*/f32[2,48,1024]{2,1,0:T(8,128)}) custom-call(bf16[128,1024]{1,0:T(8,128)(2,1)} %tok.1, bf16[128,1024]{1,0:T(8,128)(2,1)} %grd.1, s32[8,128]{1,0:T(8,128)} %bitcast.9, ...), custom_call_target="tpu_custom_call" | custom-call | tf_op jit(solution)/shard_map/pallas_call | solution.py:604
  132.9 52.9 %shard_map.119 = (bf16[128,1024]{1,0:T(8,128)(2,1)}, bf16[128,1024]{1,0:T(8,128)(2,1)}, f32[8,128]{1,0:T(8,128)}, f32[2,128,384]{2,1,0:T(8,128)}, f32[2,128,384]{2,1,0:T(8,128)}, /*index=5*/f32[2,48,1024]{2,1,0:T(8,128)}) custom-call(bf16[128,1024]{1,0:T(8,128)(2,1)} %get-tuple-element.18.refs_0_, bf16[128,1024]{1,0:T(8,128)(2,1)} %get-tuple-element.19.refs_1_, ...), custom_call_target="tpu_custom_call" | custom-call | tf_op jit(solution)/shard_map/pallas_call | solution.py:645

commit v3 on v2

--- a/solution.py
+++ b/solution.py
@@ -576,13 +576,8 @@
 
 def hand_out(*refs):
     n = len(refs) // 2
-    copies = [
-        pltpu.make_async_copy(refs[i], refs[n + i], refs[2 * n].at[i]) for i in range(n)
-    ]
-    for copy in copies:
-        copy.start()
-    for copy in copies:
-        copy.wait()
+    for i in range(n):
+        refs[n + i][...] = refs[i][...]
 
 
 def per_device(tokens, expert_ids, route_weights, out_grad, gate_weight, up_weight, down_weight):
@@ -645,9 +640,8 @@
     layer_out, token_grad, route_grad, gate_share, up_share, down_share = pl.pallas_call(
         hand_out,
         out_shape=out_shape,
-        in_specs=[hbm] * 6,
-        out_specs=(hbm,) * 6,
-        scratch_shapes=[pltpu.SemaphoreType.DMA((6,))],
+        in_specs=[vmem] * 6,
+        out_specs=(vmem,) * 6,
     )(*results)
     return (layer_out, token_grad, route_grad.T, gate_share, up_share, down_share)
 

time: 186 us -> 136 us (0.73)
  Pallas kernels: 185 us -> 135 us
    pallas_call x1, Pallas kernels: 52.9 us -> 2.6 us  [per_device(): pl.pallas_call(hand_out, out_shape=out_shape, in_specs=[vmem] * 6, out_sp...]
where the time goes in v3:
time: 136 us; the launch traced here: 135 us
  Pallas kernels  135 us (99%)
    pallas_call x1, Pallas kernels, per_device(): pl.pallas_call(kernel, out_shape=out_shape, in_specs=[vmem, vmem, vmem, v...  132 us

profile of v3, /device:TPU:1, one launch (start us, length us, event | category | flops | bytes accessed | tf_op | source)
XLA Modules:
  0.0 135.5 jit_solution(4249440044417146564)
XLA Ops:
  0.6 132.2 %shard_map.118 = (bf16[128,1024]{1,0:T(8,128)(2,1)}, bf16[128,1024]{1,0:T(8,128)(2,1)}, f32[8,128]{1,0:T(8,128)}, f32[2,128,384]{2,1,0:T(8,128)}, f32[2,128,384]{2,1,0:T(8,128)}, /*index=5*/f32[2,48,1024]{2,1,0:T(8,128)}) custom-call(bf16[128,1024]{1,0:T(8,128)(2,1)} %tok.1, bf16[128,1024]{1,0:T(8,128)(2,1)} %grd.1, s32[8,128]{1,0:T(8,128)} %bitcast.9, ...), custom_call_target="tpu_custom_call" | custom-call | tf_op jit(solution)/shard_map/pallas_call | solution.py:599
  132.9 2.6 %shard_map.119 = (bf16[128,1024]{1,0:T(8,128)(2,1)}, bf16[128,1024]{1,0:T(8,128)(2,1)}, f32[8,128]{1,0:T(8,128)}, f32[2,128,384]{2,1,0:T(8,128)}, f32[2,128,384]{2,1,0:T(8,128)}, /*index=5*/f32[2,48,1024]{2,1,0:T(8,128)}) custom-call(bf16[128,1024]{1,0:T(8,128)(2,1)} %get-tuple-element.18.refs_0_, bf16[128,1024]{1,0:T(8,128)(2,1)} %get-tuple-element.19.refs_1_, ...), custom_call_target="tpu_custom_call" | custom-call | tf_op jit(solution)/shard_map/pallas_call | solution.py:640

commit v4 on v3

--- a/solution.py
+++ b/solution.py
@@ -60,7 +60,7 @@
         self.pending, self.sent = [], 0
 
 
-N_SEND, N_RECV = 110, 210
+N_SEND, N_RECV = 99, 194
 SIGNS = (1, -1)
 LAST = ((4, 3), (3, 4))
 
@@ -149,10 +149,6 @@
         for m in range(2):
             for way in range(2):
                 x_send((m, h), way, 0, quarter[m][0].at[c, 2 * y + h], quarter[m][1].at[x, 2 * y + h])
-    for h in range(2):
-        for way in range(2):
-            part = pl.ds(4 * h, 4)
-            x_send((2, h), way, 0, gw.at[c, part], wg.at[x, part])
     for a in range(2):
         share(a, 0, firsts[a])
     local = [
@@ -319,9 +315,13 @@
             sib_tickets[a, off % NZ] = net.put(parts[a].at[p, other], sib_bufs[a].at[p], sib)
         sib_tickets[2, off % NZ] = net.put(rp.at[p, other], sib_r.at[p], sib)
 
-    z_step(0, 0)
     x_take_quarters(0)
     x_take_quarters(1)
+    for h in range(2):
+        for way in range(2):
+            part = pl.ds(4 * h, 4)
+            x_send((2, h), way, 0, gw.at[c, part], wg.at[x, part])
+    z_step(0, 0)
     for copy in local:
         copy.wait()
     z_step(1, 0)
@@ -394,7 +394,7 @@
     second = (sx, sd)
 
     def y_way(dx):
-        return 0 if dx in (2, 1) else 1
+        return 0 if dx in (2, -1) else 1
 
     def grad_send(dx):
         i = up_x(dx)
@@ -404,12 +404,6 @@
                     tickets["xf", way, g] = net.put(
                         grads[g].at[i, half[way], 0], far_x[g].at[way], dev(dx=SIGNS[way])
                     )
-            elif dx:
-                way = SIGNS.index(dx)
-                free = half[1 - way]
-                tickets["xa", way, g] = net.put(
-                    grads[g].at[i, free, 0], near_x[g].at[way, free], dev(dx=dx)
-                )
             way = y_way(dx)
             tickets["yf", dx, g] = net.put(
                 grads[g].at[i, up_y(2), 1], far_y[g].at[dx % NX], dev(dy=SIGNS[way])
@@ -429,6 +423,10 @@
             tickets["xb", way, g] = net.put(
                 mine, near_x[g].at[way, half[way]], dev(dx=SIGNS[way])
             )
+            free = half[1 - way]
+            tickets["xa", way, g] = net.put(
+                grads[g].at[i, free, 0], near_x[g].at[way, free], dev(dx=SIGNS[way])
+            )
 
     def y_pass(dx):
         way = y_way(dx)
@@ -486,41 +484,41 @@
     weight_grads(2)
     grad_send(2)
     expert(1)
+    weight_grads(1)
+    grad_send(1)
     expert(-1)
     expert(0)
     combine(4)
     combine(3)
     combine(-3)
+    y_pass(2)
     z_pass(0, 0, 0)
     z_pass(1, 1, 0)
     z_pass(0, 1, 0)
     z_pass(1, 0, 0)
-    weight_grads(1)
-    grad_send(1)
+    x_pass(0)
     weight_grads(-1)
     grad_send(-1)
-    x_pass(0)
     x_pass(1)
+    y_pass(1)
+    weight_grads(0)
+    grad_send(0)
     combine(2)
     combine(-2)
     z_pass(0, 0, 1)
     z_pass(1, 1, 1)
-    weight_grads(0)
-    grad_send(0)
     z_pass(0, 1, 1)
     z_pass(1, 0, 1)
-    y_pass(2)
-    y_pass(1)
     y_pass(-1)
     combine(1)
     combine(-1)
+    y_pass(0)
     z_pass(0, 0, 2)
     z_pass(1, 1, 2)
-    y_pass(0)
-    x_last()
     z_pass(0, 1, 2)
     z_pass(1, 0, 2)
     combine(0)
+    x_last()
     y_last()
     z_pass(0, 0, 3)
     z_pass(1, 1, 3)
@@ -634,7 +632,7 @@
         compiler_params=pltpu.CompilerParams(
             collective_id=0,
             has_side_effects=True,
-            vmem_limit_bytes=63 * 1024 * 1024,
+            vmem_limit_bytes=60 * 1024 * 1024,
         ),
     )(tokens, out_grad, expert_ids.T, route_weights.T, gate_weight, up_weight, down_weight)
     layer_out, token_grad, route_grad, gate_share, up_share, down_share = pl.pallas_call(

time: 136 us -> 127 us (0.934)
  Pallas kernels: 135 us -> 126 us
    pallas_call x1, Pallas kernels: 132 us -> 123 us  [per_device(): pl.pallas_call(kernel, out_shape=out_shape, in_specs=[vmem, vmem, vmem, v...]
where the time goes in v4:
time: 127 us
  Pallas kernels  126 us (99%)
    pallas_call x1, Pallas kernels, per_device(): pl.pallas_call(kernel, out_shape=out_shape, in_specs=[vmem, vmem, vmem, v...  123 us
    pallas_call x1, Pallas kernels, per_device(): pl.pallas_call(hand_out, out_shape=out_shape, in_specs=[vmem] * 6, out_sp...  2.6 us

profile of v4, /device:TPU:1, one launch (start us, length us, event | category | flops | bytes accessed | tf_op | source)
XLA Modules:
  0.0 126.7 jit_solution(467944689282152385)
XLA Ops:
  0.6 123.5 %shard_map.118 = (bf16[128,1024]{1,0:T(8,128)(2,1)}, bf16[128,1024]{1,0:T(8,128)(2,1)}, f32[8,128]{1,0:T(8,128)}, f32[2,128,384]{2,1,0:T(8,128)}, f32[2,128,384]{2,1,0:T(8,128)}, /*index=5*/f32[2,48,1024]{2,1,0:T(8,128)}) custom-call(bf16[128,1024]{1,0:T(8,128)(2,1)} %tok.1, bf16[128,1024]{1,0:T(8,128)(2,1)} %grd.1, s32[8,128]{1,0:T(8,128)} %bitcast.9, ...), custom_call_target="tpu_custom_call" | custom-call | tf_op jit(solution)/shard_map/pallas_call | solution.py:597
  124.1 2.6 %shard_map.119 = (bf16[128,1024]{1,0:T(8,128)(2,1)}, bf16[128,1024]{1,0:T(8,128)(2,1)}, f32[8,128]{1,0:T(8,128)}, f32[2,128,384]{2,1,0:T(8,128)}, f32[2,128,384]{2,1,0:T(8,128)}, /*index=5*/f32[2,48,1024]{2,1,0:T(8,128)}) custom-call(bf16[128,1024]{1,0:T(8,128)(2,1)} %get-tuple-element.18.refs_0_, bf16[128,1024]{1,0:T(8,128)(2,1)} %get-tuple-element.19.refs_1_, ...), custom_call_target="tpu_custom_call" | custom-call | tf_op jit(solution)/shard_map/pallas_call | solution.py:638

commit v5 on v4

--- a/solution.py
+++ b/solution.py
@@ -259,7 +259,7 @@
         scaled = (nn(pt, grd_all[p].reshape(PAIR, D)) * scale).astype(BF)
         ors[:, at, :] = scaled.reshape(NX, SLOTS, D)
 
-    def expert(dx):
+    def expert(dx, early=False):
         i = up_x(dx)
         gate_w, up_w = wg[i].reshape(D, FF), wu[i].reshape(D, FF)
         down_w = wd[i].reshape(FF, D)
@@ -269,15 +269,23 @@
         silu = gate_pre * sig
         slope = sig * (1.0 + gate_pre * (1.0 - sig))
         hidden = (silu * up_pre).astype(BF)
+        if early:
+            gd[i] = tn(hidden, outs).astype(BF).reshape(NY, 2, FF // 8, D)
+            grad_send(dx, 1)
         hidden_grad = nt(outs, down_w)
         gate_delta = (hidden_grad * up_pre * slope).astype(BF)
         up_delta = (hidden_grad * silu).astype(BF)
+        if early:
+            for m, delta in enumerate((gate_delta, up_delta)):
+                gx[i, :, :, m] = tn(rows, delta).astype(BF).reshape(NY, 2, TOK, FF)
+            grad_send(dx, 0)
         igs[i] = (nt(gate_delta, gate_w) + nt(up_delta, up_w)).astype(BF)
         expert_out = nn(hidden, down_w).astype(BF)
         wd[i] = expert_out.reshape(8, ROWS // 8, D)
-        wg[i, 0:3] = hidden.reshape(3, TOK, FF)
-        wu[i, 0:3] = gate_delta.reshape(3, TOK, FF)
-        wu[i, 3:6] = up_delta.reshape(3, TOK, FF)
+        if not early:
+            wg[i, 0:3] = hidden.reshape(3, TOK, FF)
+            wu[i, 0:3] = gate_delta.reshape(3, TOK, FF)
+            wu[i, 3:6] = up_delta.reshape(3, TOK, FF)
 
     def weight_grads(dx):
         i = up_x(dx)
@@ -396,9 +404,9 @@
     def y_way(dx):
         return 0 if dx in (2, -1) else 1
 
-    def grad_send(dx):
+    def grad_send(dx, *which):
         i = up_x(dx)
-        for g in range(2):
+        for g in which:
             if dx == 2:
                 for way in range(2):
                     tickets["xf", way, g] = net.put(
@@ -444,13 +452,15 @@
     def second_dev(h, way):
         return dev(dy=SIGNS[way]) if h == 0 else dev(dx=SIGNS[way])
 
-    def second_send(h, g):
-        way = g
+    def far_send(h, g):
         tickets["sf", h, g] = net.put(
-            second_view(h, g, 2), second[g].at[h, 2], second_dev(h, way)
+            second_view(h, g, 2), second[g].at[h, 2], second_dev(h, g)
         )
-        tickets["sn", h, g, 1 - way] = net.put(
-            second_view(h, g, SIGNS[1 - way]), second[g].at[h, 1 - way], second_dev(h, 1 - way)
+
+    def near_send(h, g):
+        way = 1 - g
+        tickets["sn", h, g, way] = net.put(
+            second_view(h, g, SIGNS[way]), second[g].at[h, way], second_dev(h, way)
         )
 
     def x_last():
@@ -459,16 +469,19 @@
                 net.got(tickets["xa", way, g], near_x[g].at[way, half[1 - way]])
                 net.got(tickets["xb", way, g], near_x[g].at[way, half[way]])
             add(grads[g].at[x, :, 0], near_x[g].at[0], near_x[g].at[1])
-            second_send(0, g)
-
-    def y_last():
+            far_send(0, g)
+            near_send(0, g)
+
+    def y_last(dx):
         for g in range(2):
-            for dx in (2, 1, -1, 0):
-                for way in range(2):
-                    net.got(tickets["yn", dx, way, g], near_y[g].at[dx % NX, way])
-                near = near_y[g].at[dx % NX]
-                add(grads[g].at[up_x(dx), y, 1], near.at[0], near.at[1])
-            second_send(1, g)
+            for way in range(2):
+                net.got(tickets["yn", dx, way, g], near_y[g].at[dx % NX, way])
+            near = near_y[g].at[dx % NX]
+            add(grads[g].at[up_x(dx), y, 1], near.at[0], near.at[1])
+            if dx == 2:
+                far_send(1, g)
+            elif dx == SIGNS[1 - g]:
+                near_send(1, g)
 
     def second_pass(h):
         for g in range(2):
@@ -480,12 +493,8 @@
                 mine, second[g].at[h, way], second_dev(h, way)
             )
 
-    expert(2)
-    weight_grads(2)
-    grad_send(2)
-    expert(1)
-    weight_grads(1)
-    grad_send(1)
+    expert(2, early=True)
+    expert(1, early=True)
     expert(-1)
     expert(0)
     combine(4)
@@ -498,11 +507,11 @@
     z_pass(1, 0, 0)
     x_pass(0)
     weight_grads(-1)
-    grad_send(-1)
+    grad_send(-1, 0, 1)
     x_pass(1)
     y_pass(1)
     weight_grads(0)
-    grad_send(0)
+    grad_send(0, 0, 1)
     combine(2)
     combine(-2)
     z_pass(0, 0, 1)
@@ -513,17 +522,20 @@
     combine(1)
     combine(-1)
     y_pass(0)
+    y_last(2)
     z_pass(0, 0, 2)
     z_pass(1, 1, 2)
+    y_last(1)
     z_pass(0, 1, 2)
     z_pass(1, 0, 2)
     combine(0)
+    y_last(-1)
     x_last()
-    y_last()
+    second_pass(1)
     z_pass(0, 0, 3)
     z_pass(1, 1, 3)
+    y_last(0)
     second_pass(0)
-    second_pass(1)
 
     results = (lo, tg)
     for a in range(2):
@@ -597,7 +609,7 @@
     results = pl.pallas_call(
         kernel,
         out_shape=out_shape,
-        in_specs=[vmem, vmem, vmem, vmem, hbm, hbm, hbm],
+        in_specs=[hbm, hbm, vmem, vmem, hbm, hbm, hbm],
         out_specs=(vmem,) * 6,
         scratch_shapes=[
             pltpu.VMEM((NZ, NC, TOK, D), BF),
@@ -632,7 +644,7 @@
         compiler_params=pltpu.CompilerParams(
             collective_id=0,
             has_side_effects=True,
-            vmem_limit_bytes=60 * 1024 * 1024,
+            vmem_limit_bytes=63 * 1024 * 1024,
         ),
     )(tokens, out_grad, expert_ids.T, route_weights.T, gate_weight, up_weight, down_weight)
     layer_out, token_grad, route_grad, gate_share, up_share, down_share = pl.pallas_call(

time: 127 us -> 124 us (0.976)
  Pallas kernels: 126 us -> 123 us
    pallas_call x1, Pallas kernels: 123 us -> 121 us  [per_device(): pl.pallas_call(kernel, out_shape=out_shape, in_specs=[hbm, hbm, vmem, vme...]
where the time goes in v5:
time: 124 us
  Pallas kernels  123 us (99%)
    pallas_call x1, Pallas kernels, per_device(): pl.pallas_call(kernel, out_shape=out_shape, in_specs=[hbm, hbm, vmem, vme...  121 us
    pallas_call x1, Pallas kernels, per_device(): pl.pallas_call(hand_out, out_shape=out_shape, in_specs=[vmem] * 6, out_sp...  2.6 us

profile of v5, /device:TPU:1, one launch (start us, length us, event | category | flops | bytes accessed | tf_op | source)
XLA Modules:
  0.0 124.1 jit_solution(2980596600149381996)
XLA Ops:
  0.6 120.8 %shard_map.118 = (bf16[128,1024]{1,0:T(8,128)(2,1)}, bf16[128,1024]{1,0:T(8,128)(2,1)}, f32[8,128]{1,0:T(8,128)}, f32[2,128,384]{2,1,0:T(8,128)}, f32[2,128,384]{2,1,0:T(8,128)}, /*index=5*/f32[2,48,1024]{2,1,0:T(8,128)}) custom-call(bf16[128,1024]{1,0:T(8,128)(2,1)} %tok.1, bf16[128,1024]{1,0:T(8,128)(2,1)} %grd.1, s32[8,128]{1,0:T(8,128)} %bitcast.9, ...), custom_call_target="tpu_custom_call" | custom-call | tf_op jit(solution)/shard_map/pallas_call | solution.py:609
  121.5 2.6 %shard_map.119 = (bf16[128,1024]{1,0:T(8,128)(2,1)}, bf16[128,1024]{1,0:T(8,128)(2,1)}, f32[8,128]{1,0:T(8,128)}, f32[2,128,384]{2,1,0:T(8,128)}, f32[2,128,384]{2,1,0:T(8,128)}, /*index=5*/f32[2,48,1024]{2,1,0:T(8,128)}) custom-call(bf16[128,1024]{1,0:T(8,128)(2,1)} %get-tuple-element.18.refs_0_, bf16[128,1024]{1,0:T(8,128)(2,1)} %get-tuple-element.19.refs_1_, ...), custom_call_target="tpu_custom_call" | custom-call | tf_op jit(solution)/shard_map/pallas_call | solution.py:650

commit v6 on v5

--- a/solution.py
+++ b/solution.py
@@ -60,7 +60,7 @@
         self.pending, self.sent = [], 0
 
 
-N_SEND, N_RECV = 99, 194
+N_SEND, N_RECV = 95, 180
 SIGNS = (1, -1)
 LAST = ((4, 3), (3, 4))
 
@@ -145,10 +145,10 @@
         rings_x[name, way, s] = net.put(src, dst, dev(dx=SIGNS[way]))
 
     quarter = ((uw, wu), (dw, wd))
-    for h in range(2):
-        for m in range(2):
-            for way in range(2):
-                x_send((m, h), way, 0, quarter[m][0].at[c, 2 * y + h], quarter[m][1].at[x, 2 * y + h])
+    mine = pl.ds(2 * y, 2)
+    for m in range(2):
+        for way in range(2):
+            x_send(m, way, 0, quarter[m][0].at[c, mine], quarter[m][1].at[x, mine])
     for a in range(2):
         share(a, 0, firsts[a])
     local = [
@@ -173,14 +173,13 @@
 
     def x_take_quarters(way):
         d = SIGNS[way]
-        for h in range(2):
-            for m in range(2):
-                piece = quarter[m][1].at[up_x(-d), 2 * y + h]
-                net.got(rings_x[(m, h), way, 0], piece)
-                if h == way:
-                    x_send((m, h), way, 1, piece, piece)
-                for to in range(2):
-                    y_send((m, h, -d), to, 0, piece)
+        for m in range(2):
+            both = quarter[m][1].at[up_x(-d), mine]
+            net.got(rings_x[m, way, 0], both)
+            piece = quarter[m][1].at[up_x(-d), 2 * y + way]
+            x_send((m, way), way, 1, piece, piece)
+            for to in range(2):
+                y_send((m, -d), to, 0, both)
 
     def x_take_far():
         for m in range(2):
@@ -193,9 +192,14 @@
     def y_take(dx):
         for m in range(2):
             for way in range(2):
+                first = 2 * up_y(-SIGNS[way])
+                if dx != 2:
+                    both = quarter[m][1].at[up_x(dx), pl.ds(first, 2)]
+                    net.got(rings_y[(m, dx), way, 0], both)
                 for h in range(2):
-                    piece = quarter[m][1].at[up_x(dx), 2 * up_y(-SIGNS[way]) + h]
-                    net.got(rings_y[(m, h, dx), way, 0], piece)
+                    piece = quarter[m][1].at[up_x(dx), first + h]
+                    if dx == 2:
+                        net.got(rings_y[(m, h, dx), way, 0], piece)
                     if h == way:
                         y_send((m, h, dx), way, 1, piece)
 
@@ -207,11 +211,9 @@
 
     def x_take_gate():
         for way in range(2):
-            for h in range(2):
-                piece = wg.at[up_x(-SIGNS[way]), pl.ds(4 * h, 4)]
-                net.got(rings_x[(2, h), way, 0], piece)
-                if h == way:
-                    x_send((2, h), way, 1, piece, piece)
+            net.got(rings_x[2, way, 0], wg.at[up_x(-SIGNS[way])])
+            piece = wg.at[up_x(-SIGNS[way]), pl.ds(4 * way, 4)]
+            x_send((2, way), way, 1, piece, piece)
 
     def x_take_gate_far():
         for way in range(2):
@@ -325,10 +327,8 @@
 
     x_take_quarters(0)
     x_take_quarters(1)
-    for h in range(2):
-        for way in range(2):
-            part = pl.ds(4 * h, 4)
-            x_send((2, h), way, 0, gw.at[c, part], wg.at[x, part])
+    for way in range(2):
+        x_send(2, way, 0, gw.at[c], wg.at[x])
     z_step(0, 0)
     for copy in local:
         copy.wait()

time: 124 us -> 126 us (1.016)
  Pallas kernels: 123 us -> 125 us
    pallas_call x1, Pallas kernels: 121 us -> 122 us  [per_device(): pl.pallas_call(kernel, out_shape=out_shape, in_specs=[hbm, hbm, vmem, vme...]
where the time goes in v6:
time: 126 us
  Pallas kernels  125 us (99%)
    pallas_call x1, Pallas kernels, per_device(): pl.pallas_call(kernel, out_shape=out_shape, in_specs=[hbm, hbm, vmem, vme...  122 us
    pallas_call x1, Pallas kernels, per_device(): pl.pallas_call(hand_out, out_shape=out_shape, in_specs=[vmem] * 6, out_sp...  2.6 us

profile of v6, /device:TPU:1, one launch (start us, length us, event | category | flops | bytes accessed | tf_op | source)
XLA Modules:
  0.0 125.7 jit_solution(13580652176218883415)
XLA Ops:
  0.6 122.4 %shard_map.118 = (bf16[128,1024]{1,0:T(8,128)(2,1)}, bf16[128,1024]{1,0:T(8,128)(2,1)}, f32[8,128]{1,0:T(8,128)}, f32[2,128,384]{2,1,0:T(8,128)}, f32[2,128,384]{2,1,0:T(8,128)}, /*index=5*/f32[2,48,1024]{2,1,0:T(8,128)}) custom-call(bf16[128,1024]{1,0:T(8,128)(2,1)} %tok.1, bf16[128,1024]{1,0:T(8,128)(2,1)} %grd.1, s32[8,128]{1,0:T(8,128)} %bitcast.9, ...), custom_call_target="tpu_custom_call" | custom-call | tf_op jit(solution)/shard_map/pallas_call | solution.py:609
  123.1 2.6 %shard_map.119 = (bf16[128,1024]{1,0:T(8,128)(2,1)}, bf16[128,1024]{1,0:T(8,128)(2,1)}, f32[8,128]{1,0:T(8,128)}, f32[2,128,384]{2,1,0:T(8,128)}, f32[2,128,384]{2,1,0:T(8,128)}, /*index=5*/f32[2,48,1024]{2,1,0:T(8,128)}) custom-call(bf16[128,1024]{1,0:T(8,128)(2,1)} %get-tuple-element.18.refs_0_, bf16[128,1024]{1,0:T(8,128)(2,1)} %get-tuple-element.19.refs_1_, ...), custom_call_target="tpu_custom_call" | custom-call | tf_op jit(solution)/shard_map/pallas_call | solution.py:650
